TPU v7x, 32 devices: a whole 2x2x4 slice. The times are simulated.
32 devices in a mesh: row: 4 (over y, x), col: 8 (over z, core).
Axes of the slice: x: 2, y: 2, z: 4, core: 2. Of those that a mesh axis runs over, the one named last changes fastest.
Arguments:
- amplitudes: float32 [128, 128, 6144], P('col', 'row'), may hold values from -6 to 6
- integrals: float32 [6144, 6144], P('col', 'row'), may hold values from -0.078125 to 0.078125
- amp_pattern: int32 [128, 48], P('col'), may hold values 0 or 1
- int_pattern: int32 [48, 48], P(None, 'row'), may hold values from 0 to 1
Outputs:
- ladder: float32 [128, 128, 6144], P('col', 'row')
All inputs are finite; a program needn't handle non-finite values. No bound on the sum of `amp_pattern` on one device may be relied on, other than what follows from the above.
Results may differ from a plain program's by a relative error of at most 0.00007.
Values sent between devices are 32-bit elements; how exact they have to be, the bound alone decides.
No kernel may reach another device: no remote copies, remote signals or barrier semaphores. Data moves between devices by JAX's collectives and lax.ppermute only.
A program may use at most 256 MiB of HBM per device.

v0:
```python
import functools

import jax
import jax.numpy as jnp
from jax import lax
from jax.experimental import pallas as pl
from jax.experimental.pallas import tpu as pltpu
from jax.sharding import PartitionSpec as P

TILE = 128
CORES = 2
UNROLL = 3
VMEM_LIMIT = 48 * 1024 * 1024


def split_kernel(mine_pattern, other_pattern, mine_ref, other_ref, out_ref, *cleared, second, deep):
    rows = mine_ref.shape[0]
    for ref in cleared:
        ref[...] = jnp.zeros_like(ref)
    for i in range(deep):
        k = pl.program_id(0) * deep + i
        lanes = pl.ds(i * TILE, TILE)
        for half, (pattern, amp_ref) in enumerate(((mine_pattern, mine_ref), (other_pattern, other_ref))):
            for first in range(rows // second):
                value = amp_ref[pl.ds(first * second, second), lanes] * pattern[first, k].astype(jnp.float32)
                high = value.astype(jnp.bfloat16)
                low = (value - high.astype(jnp.float32)).astype(jnp.bfloat16)
                here = pl.ds(half * rows + first * second, second)
                out_ref[i, here, :TILE] = high
                out_ref[i, here, TILE:] = low


def split_amplitudes(mine, other, mine_pattern, other_pattern, second, blocks):
    rows, depth = mine.shape
    tiles = depth // TILE
    deep = 4 if tiles % 4 == 0 else 1
    steps = tiles // deep
    out_shape = [jax.ShapeDtypeStruct((tiles, CORES * rows, 2 * TILE), jnp.bfloat16)]
    out_specs = [pl.BlockSpec((deep, CORES * rows, 2 * TILE), lambda k, *_: (k, 0, 0))]
    if blocks % steps == 0:
        out_shape.append(jax.ShapeDtypeStruct((rows, blocks * TILE), jnp.float32))
        out_specs.append(pl.BlockSpec((rows, blocks // steps * TILE), lambda k, *_: (0, k)))
    made = pl.pallas_call(
        functools.partial(split_kernel, second=second, deep=deep),
        grid_spec=pltpu.PrefetchScalarGridSpec(
            num_scalar_prefetch=2,
            grid=(steps,),
            in_specs=[pl.BlockSpec((rows, deep * TILE), lambda k, *_: (0, k))] * 2,
            out_specs=out_specs,
        ),
        out_shape=out_shape,
        compiler_params=pltpu.CompilerParams(vmem_limit_bytes=VMEM_LIMIT),
        cost_estimate=pl.CostEstimate(flops=8 * rows * depth, bytes_accessed=20 * rows * depth, transcendentals=0),
    )(mine_pattern, other_pattern, mine, other)
    return made if len(made) == 2 else (made[0], jnp.zeros((rows, blocks * TILE), jnp.float32))


def pack_kernel(source_ref, row_ref, lane_ref, *refs, plan, sources):
    ins, outs = refs[:sources], refs[sources:]
    for out, (base, size) in zip(outs, plan):

        def copy(slot, _, out=out, base=base):
            row = pl.multiple_of(row_ref[base + slot], TILE)
            lane = pl.multiple_of(lane_ref[base + slot], TILE)
            for source in range(sources):

                @pl.when(source_ref[base + slot] == source)
                def _(source=source):
                    out[slot] = ins[source][pl.ds(row, TILE), pl.ds(lane, TILE)]

            return 0

        lax.fori_loop(0, size, copy, 0)


def pack(scalars, sources, plan):
    whole = lambda x: pl.BlockSpec(x.shape, lambda g, *s: (0,) * len(x.shape))
    outs = [jax.ShapeDtypeStruct((size, TILE, TILE), jnp.float32) for _, size in plan]
    return pl.pallas_call(
        functools.partial(pack_kernel, plan=plan, sources=len(sources)),
        grid_spec=pltpu.PrefetchScalarGridSpec(
            num_scalar_prefetch=len(scalars),
            grid=(1,),
            in_specs=[whole(x) for x in sources],
            out_specs=[whole(x) for x in outs],
        ),
        out_shape=outs,
        compiler_params=pltpu.CompilerParams(vmem_limit_bytes=VMEM_LIMIT),
        cost_estimate=pl.CostEstimate(
            flops=0, bytes_accessed=4 * (sum(x.size for x in sources) + sum(x.size for x in outs)), transcendentals=0
        ),
    )(*scalars, *sources)


def pool_kernel(sizes_ref, offsets_ref, *refs):
    *ins, out = refs
    for e, ref in enumerate(ins):

        def copy(slot, _, ref=ref, e=e):
            out[offsets_ref[e] + slot] = ref[slot]
            return 0

        lax.fori_loop(0, sizes_ref[e], copy, 0)


def pool(sizes, offsets, lists, capacity):
    whole = lambda shape: pl.BlockSpec(shape, lambda g, *s: (0,) * len(shape))
    shape = (capacity, TILE, TILE)
    return pl.pallas_call(
        pool_kernel,
        grid_spec=pltpu.PrefetchScalarGridSpec(
            num_scalar_prefetch=2,
            grid=(1,),
            in_specs=[whole(x.shape) for x in lists],
            out_specs=whole(shape),
        ),
        out_shape=jax.ShapeDtypeStruct(shape, jnp.float32),
        compiler_params=pltpu.CompilerParams(vmem_limit_bytes=VMEM_LIMIT),
        cost_estimate=pl.CostEstimate(flops=0, bytes_accessed=12 * capacity * TILE * TILE, transcendentals=0),
    )(sizes, offsets, *lists)


def gate_kernel(*refs):
    del refs


def gate(released, awaited):
    anywhere = pl.BlockSpec(memory_space=pl.ANY)
    return pl.pallas_call(
        gate_kernel,
        in_specs=[anywhere] * (len(released) + len(awaited)),
        out_specs=[anywhere] * len(released),
        out_shape=[jax.ShapeDtypeStruct(x.shape, x.dtype) for x in released],
        input_output_aliases={i: i for i in range(len(released))},
    )(*released, *awaited)


def multiply_kernel(
    plane_ref, low_ref, high_ref, shift_ref, base_ref, mine_at, other_at, kk_ref, amp_ref, mine_in, other_in, *refs,
    segments, steps, per_chip, wide,
):
    count = len(segments)
    tiles = refs[:count]
    mine_ref, other_ref, buffer, sem = refs[count:]
    step = pl.program_id(0)
    rows = mine_ref.shape[0]

    def issue(g, half):
        low, high = low_ref[g * wide], high_ref[g * wide + wide - 1]
        for ref, (a, b, pooled, only) in zip(tiles, segments):
            shift = shift_ref[g * wide] if pooled else -a

            def start(slot, _, ref=ref, shift=shift):
                pltpu.make_async_copy(
                    ref.at[slot + shift], buffer.at[half, slot - low], sem.at[half, slot - low]
                ).start()
                return 0

            first = jnp.maximum(low, a)
            last = jnp.maximum(first, jnp.minimum(high, b))
            if only is not None:
                last = jnp.where(g * wide // per_chip == only, last, first)
            lax.fori_loop(first, last, start, 0)

    half = lax.rem(step, 2)

    @pl.when(step == 0)
    def _():
        issue(0, 0)

    @pl.when(step + 1 < steps)
    def _():
        issue(step + 1, 1 - half)

    mine_ref[...] = mine_in[...]
    other_ref[...] = other_in[...]
    origin = low_ref[step * wide]
    for i in range(wide):
        lanes = pl.ds(i * TILE, TILE)
        low = low_ref[step * wide + i]
        length = high_ref[step * wide + i] - low
        base = base_ref[step * wide] + low

        def wait(at, _, low=low):
            at = low - origin + at
            pltpu.make_async_copy(tiles[0].at[0], buffer.at[half, at], sem.at[half, at]).wait()
            return 0

        lax.fori_loop(0, length, wait, 0)

        def add(turn, _, lanes=lanes, low=low, length=length, base=base):
            weights, ks = [], []
            for u in range(UNROLL):
                at = turn * UNROLL + u
                inside = at < length
                at = jnp.minimum(at, length - 1)
                value = buffer[half, low - origin + at]
                if u:
                    value = jnp.where(inside, value, 0.0)
                high = value.astype(jnp.bfloat16)
                rest = (value - high.astype(jnp.float32)).astype(jnp.bfloat16)
                weights.append(jnp.concatenate([high, rest], axis=1))
                weights.append(jnp.concatenate([high, jnp.zeros_like(high)], axis=1))
                ks.append(kk_ref[base + at])
            left = jnp.concatenate([amp_ref[k] for k in ks], axis=1)
            product = jnp.dot(left, jnp.concatenate(weights, axis=0), preferred_element_type=jnp.float32)
            total = product[:, :TILE] + product[:, TILE:]
            mine_ref[:, lanes] += total[:rows]
            other_ref[:, lanes] += total[rows:]
            return 0

        lax.fori_loop(0, (length + UNROLL - 1) // UNROLL, add, 0)


def multiply(scalars, steps, per_chip, wide, amps, mine, other, pieces, kd):
    rows = mine.shape[0]
    segments = [piece[1:] for piece in pieces]
    expected = 10 * steps * wide
    n = len(scalars)
    mine_spec = pl.BlockSpec((rows, wide * TILE), lambda g, *s: (0, s[5][g]))
    other_spec = pl.BlockSpec((rows, wide * TILE), lambda g, *s: (0, s[6][g]))
    anywhere = pl.BlockSpec(memory_space=pl.ANY)
    held = CORES * kd * wide
    return pl.pallas_call(
        functools.partial(multiply_kernel, segments=segments, steps=steps, per_chip=per_chip, wide=wide),
        grid_spec=pltpu.PrefetchScalarGridSpec(
            num_scalar_prefetch=n,
            grid=(steps,),
            in_specs=[
                pl.BlockSpec((CORES * kd, CORES * rows, 2 * TILE), lambda g, *s: (s[0][0], 0, 0)),
                mine_spec,
                other_spec,
            ]
            + [anywhere] * len(pieces),
            out_specs=[mine_spec, other_spec],
            scratch_shapes=[pltpu.VMEM((2, held, TILE, TILE), jnp.float32), pltpu.SemaphoreType.DMA((2, held))],
        ),
        out_shape=[jax.ShapeDtypeStruct(x.shape, x.dtype) for x in (mine, other)],
        input_output_aliases={n + 1: 0, n + 2: 1},
        compiler_params=pltpu.CompilerParams(vmem_limit_bytes=VMEM_LIMIT),
        cost_estimate=pl.CostEstimate(
            flops=expected * 32 * rows * TILE * TILE,
            bytes_accessed=expected * 4 * TILE * TILE,
            transcendentals=0,
        ),
    )(*scalars, amps, mine, other, *[piece[0] for piece in pieces])


def place_kernel(at_ref, mine_in, piece_ref, out_ref):
    out_ref[...] = mine_in[...] + piece_ref[...]


def place(at, wide, mine, piece):
    rows = mine.shape[0]
    spec = pl.BlockSpec((rows, wide * TILE), lambda g, a: (0, a[g]))
    return pl.pallas_call(
        place_kernel,
        grid_spec=pltpu.PrefetchScalarGridSpec(
            num_scalar_prefetch=1,
            grid=(at.shape[0],),
            in_specs=[spec, pl.BlockSpec((rows, wide * TILE), lambda g, a: (0, g))],
            out_specs=spec,
        ),
        out_shape=jax.ShapeDtypeStruct(mine.shape, mine.dtype),
        input_output_aliases={1: 0},
        compiler_params=pltpu.CompilerParams(vmem_limit_bytes=VMEM_LIMIT),
        cost_estimate=pl.CostEstimate(flops=piece.size, bytes_accessed=12 * piece.size, transcendentals=0),
    )(at, mine, piece)


def body(amplitudes, integrals, amp_pattern, int_pattern, *, chips, devices):
    R, Z = chips, devices // CORES
    first, second, depth = amplitudes.shape
    rows = first * second
    kd = integrals.shape[0] // TILE
    ntl = integrals.shape[1] // TILE
    groups = R if ntl % R == 0 else 1
    width = ntl // groups
    if groups == 4:
        wide = width
        owned = [[d * width + i for d in pair for i in range(width)] for pair in ((0, 3), (1, 2))]
    else:
        wide = 1
        owned = [list(range(c, ntl, CORES)) for c in range(CORES)]
        owned = [x + [ntl] * (len(owned[0]) - len(x)) for x in owned]
    per_chip = len(owned[0])
    tiles = per_chip * CORES * kd

    r = lax.axis_index("row")
    col = lax.axis_index("col")
    core = lax.rem(col, CORES)
    ring = [0] + list(range(1, Z, 2)) + [z for z in range(Z - 1, 0, -1) if z % 2 == 0]
    spot = [ring.index(z) for z in range(Z)]

    def by_row(x, distance):
        return lax.ppermute(x, "row", [(a, a ^ distance) for a in range(R)])

    def by_core(x):
        return lax.ppermute(x, "col", [(a, a ^ 1) for a in range(Z * CORES)])

    def by_plane(x):
        return lax.ppermute(
            x,
            "col",
            [(ring[a] * CORES + c, ring[(a + 1) % Z] * CORES + c) for a in range(Z) for c in range(CORES)],
        )

    blocks = R * ntl
    spare = per_chip * CORES - ntl
    parts_of = [[0], [1, 2], [3]] if R == 4 else [list(range(R))]
    others = [jnp.zeros((rows, len(part) * per_chip * TILE), jnp.float32) for part in parts_of]
    shares = [integrals[:, d * width * TILE : (d + 1) * width * TILE] for d in range(groups)]
    if groups > 1:
        (int_pattern,) = gate([int_pattern], shares[1:])
    for d in range(1, groups):
        shares[d] = by_row(shares[d], d)

    amps_mine = amplitudes.reshape(rows, depth)
    amps, mine = split_amplitudes(
        amps_mine, by_core(amps_mine), amp_pattern, by_core(amp_pattern), second, blocks + spare
    )
    if groups > 1:
        shares[1:] = gate(shares[1:], [amps])
    twins = [by_core(x) for x in shares]

    patterns = [int_pattern] + [by_row(int_pattern, d) for d in range(1, R)]
    by_distance = jnp.stack(patterns).reshape(R, Z, CORES * kd, groups, width)
    near = []
    for e in range(R):
        picked = jnp.stack([by_distance[e ^ d, :, :, d] for d in range(groups)], axis=2)
        near.append(picked.reshape(Z, CORES * kd, ntl))
    present = (jnp.stack(near, axis=1) != 0).astype(jnp.int32)
    present = jnp.pad(present, ((0, 0), (0, 0), (0, 0), (0, per_chip * CORES - ntl)))
    present = jnp.stack([jnp.stack([present[..., j] for j in x], axis=-1) for x in owned], axis=-1)
    present = present.transpose(0, 1, 4, 3, 2)
    both = present.reshape(Z, R, CORES, tiles)
    cores_counts = jnp.sum(both, axis=-1)
    own = jnp.where(core == 0, both[:, :, 0], both[:, :, 1])
    here = jnp.asarray(spot)[col // CORES]
    planes = jnp.asarray(ring)[lax.rem(here - jnp.arange(Z) + Z, Z)]
    if R == 4:
        own = jnp.stack(
            [
                own[:, 0],
                jnp.where(core == 0, own[:, 1], own[:, 2]),
                jnp.where(core == 0, own[:, 2], own[:, 1]),
                own[:, 3],
            ],
            axis=1,
        )
    own = own[planes]
    counts = jnp.sum(own, axis=-1)
    ids = jnp.arange(tiles)
    slot_of = jnp.sum(own[..., None, :] * (ids[None, :] < ids[:, None]), axis=-1)
    slots = (
        jnp.sum(
            (ids + 1)[None, None, None, :]
            * ((slot_of[:, :, None, :] == ids[:, None]) & (own[:, :, None, :] > 0)),
            axis=-1,
        )
        - 1
    )
    ends = jnp.sum(own[:, :, None, :] * (ids[None, :] < (jnp.arange(per_chip + 1) * CORES * kd)[:, None]), axis=-1)

    straight = max(2, round(tiles * 35 / 72)) if R == 4 else max(4, 2 * round(tiles * 25 / 72))
    extra = max(2, round(tiles * 16 / 72)) if R == 4 else 0
    pooled = max(R, round(tiles * 32 / 72)) if R == 4 else 0
    longest = tiles + straight + extra
    slots = jnp.pad(slots, ((0, 0), (0, 0), (0, longest - tiles)), constant_values=-1)
    most = jnp.max(cores_counts)

    def chips_of(which):
        return r ^ (jnp.stack([0 * which, 1 + which, 2 - which, 0 * which + 3]) if R == 4 else jnp.arange(R))

    chip_of = chips_of(core)

    def columns_of(which):
        column = jnp.asarray(owned)[which][None, ::wide]
        group = column // width
        chip = chips_of(which)[:, None]
        at = (((chip ^ group) if groups > 1 else chip) * groups + group) * width + column % width
        return (jnp.where(column < ntl, at, blocks) // wide).astype(jnp.int32)

    mine_at = columns_of(core)
    received_at = columns_of(1 - core)

    def across(x, near):
        return lax.ppermute(
            x,
            ("row", "col"),
            [
                (a * devices + d, (a ^ (near if d % CORES == 0 else 3 - near)) * devices + d)
                for a in range(R)
                for d in range(devices)
            ],
        )

    def one_round(state, others):
        base, mine = state
        others = list(others)
        after = base + straight
        left = jnp.clip(cores_counts - after, 0, extra)
        fits = jnp.max(jnp.sum(left, axis=1)) <= pooled
        taken = jnp.where(fits, extra, pooled // R) if extra else jnp.int32(0)
        sizes = jnp.clip(counts - after, 0, taken)
        before = chip_of[None, :] < chip_of[:, None]
        offsets = jnp.sum(sizes[:, None, :] * before[None], axis=-1).astype(jnp.int32)
        now = lax.dynamic_slice_in_dim(slots, base, straight + extra, axis=2)
        kk = jnp.maximum(now, 0) % (CORES * kd)
        bounds = jnp.clip(ends - base, 0, straight + taken).astype(jnp.int32)

        column = jnp.asarray(owned)[core][jnp.maximum(now[0, 0], 0) // (CORES * kd)]
        holder = kk[0, 0] // kd
        source = jnp.where(now[0, 0] < 0, -1, (holder != core) * groups + column // width)
        where = [source, kk[0, 0] % kd * TILE, column % width * TILE]
        plan = ((0, straight), (straight, extra), (0, straight)) if extra else ((0, straight),)
        packed = pack([x.astype(jnp.int32) for x in where], shares + twins, plan)


        def add(mine, other, step, neighbours, low_slot, high_slot, pieces, spot=0):
            low, high, shift, base_at = [], [], [], []
            for e in neighbours:
                limits = jnp.clip(bounds[step, e], low_slot, high_slot)
                low.append(limits[:-1])
                high.append(limits[1:])
                shift.append(jnp.broadcast_to(offsets[step, e] - straight, (per_chip,)))
                base_at.append(jnp.full((per_chip,), (e - neighbours[0]) * (straight + extra)))
            first_e, last_e = neighbours[0], neighbours[-1] + 1
            lists = [jnp.concatenate(x) for x in (low, high, shift, base_at)]
            lists.append(mine_at[first_e:last_e].reshape(-1))
            steps = len(neighbours) * per_chip // wide
            lists.append(jnp.arange(steps) + spot * per_chip // wide)
            scalars = [planes[step].reshape(1), *lists, kk[step, first_e:last_e].reshape(-1)]
            scalars = [x.astype(jnp.int32) for x in scalars]
            return multiply(scalars, steps, per_chip, wide, amps, mine, other, pieces, kd)

        if R == 4:
            end = straight + extra
            sent, late, ready = packed
            along = [sent, by_plane(sent)]
            first_late, second_late = across(late, 1), across(late, 2)
            at_home = [(sent, 0, straight, False, None), (late, straight, end, False, None)]
            mine, others[0] = add(mine, others[0], 0, [0], 0, end, at_home)
            first_late, ready, mine = gate([first_late, ready, mine], [second_late])
            third_late = across(first_late, 2)
            first_near, second_near = across(ready, 1), across(ready, 2)
            pools = [
                pool(
                    sizes[0].astype(jnp.int32),
                    offsets[0],
                    [late, first_late, second_late, third_late],
                    pooled,
                )
            ]
            pools.append(by_plane(pools[0]))
            received = []
            for step in range(Z):
                first_near, mine = gate([first_near, mine], [second_near, pools[step]])
                third_near = across(first_near, 2)
                mixed = (pools[step], straight, end, True, None)
                near = [(first_near, 0, straight, False, 0), (second_near, 0, straight, False, 1), mixed]
                last = [(third_near, 0, straight, False, None), mixed]
                if step:
                    home = [(along[step], 0, straight, False, None), mixed]
                    mine, others[0] = add(mine, others[0], step, [0], 0, end, home)
                if step == Z - 1:
                    received.append(by_core(others[0]))
                else:
                    along[step + 1], mine = gate([along[step + 1], mine], [third_near])
                    first_near, second_near = across(along[step + 1], 1), across(along[step + 1], 2)
                    if step + 2 < Z:
                        along.append(by_plane(along[step + 1]))
                        pools.append(by_plane(pools[step + 1]))
                mine, others[1] = add(mine, others[1], step, [1, 2], 0, end, near)
                if step == Z - 1:
                    received.append(by_core(others[1]))
                    mine = place(received_at[0], wide, mine, received[0])
                mine, others[2] = add(mine, others[2], step, [3], 0, end, last)
            received.append(by_core(others[2]))
            mine = place(received_at[1:3].reshape(-1), wide, mine, received[1])
            mine = place(received_at[3], wide, mine, received[2])
        else:
            now_at = packed[0]
            for step in range(Z):
                for e in range(R):
                    piece = by_row(now_at, e) if e else now_at
                    mine, others[0] = add(mine, others[0], step, [e], 0, straight, [(piece, 0, straight, False, None)], e)
                if step + 1 < Z:
                    now_at = by_plane(now_at)
            mine = place(received_at.reshape(-1), wide, mine, by_core(others[0]))
        return base + straight + taken, mine

    state = one_round((jnp.int32(0), mine), others)
    cleared = [x.shape for x in others]
    _, mine = lax.while_loop(
        lambda state: state[0] < most,
        lambda state: one_round(state, [jnp.zeros(shape, jnp.float32) for shape in cleared]),
        state,
    )
    return mine[:, : blocks * TILE].reshape(first, second, blocks * TILE)


def solution(mesh):
    placed = (P("col", "row", None), P("col", "row"), P("col", None), P(None, "row"))
    return jax.shard_map(
        functools.partial(body, chips=mesh.shape["row"], devices=mesh.shape["col"]),
        mesh=mesh,
        in_specs=placed,
        out_specs=P("col", "row", None),
        check_vma=False,
    )
```

profile of v0, /device:TPU:0, one launch (start us, length us, event | category | flops | bytes accessed | tf_op | source)
XLA Modules:
  0.0 525.5 jit_solution(8887461146190538090)
XLA Ops:
  1.8 4.6 fusion.27
  26.9 24.4 %shard_map.101 = (bf16[48,1024,256]{2,1,0:T(8,128)(2,1)}, f32[512,6144]{1,0:T(8,128)}) custom-call(s32[16,48]{1,0:T(8,128)S(1)} %copy-done.28, s32[16,48]{1,0:T(8,128)S(1)} %collective-permute-done.27.other_pattern, f32[512,6144]{1,0:T(8,128)} %bitcast.364, f32[512,6144]{1,0:T(8,128)} %collective-permute-done.28.other_ref), custom_call_target="tpu_custom_call" | custom-call | flops 25165824 | bytes 62914560 | tf_op jit(solution)/shard_map/pallas_call | solution.py:43
  51.3 19.0 %collective-permute-done.30.refs_1_ = f32[768,384]{1,0:T(8,128)S(1)} collective-permute-done((f32[768,384]{1,0:T(8,128)}, f32[768,384]{1,0:T(8,128)S(1)}, u32[]{:S(2)}, u32[]{:S(2)}) %collective-permute-start.30) | collective-permute-done | bytes 1179680 | tf_op jit(solution)/shard_map/ppermute | solution.py:296
  76.8 9.5 %shard_map.103 = (f32[35,128,128]{2,1,0:T(8,128)S(1)}, f32[16,128,128]{2,1,0:T(8,128)S(1)}, f32[35,128,128]{2,1,0:T(8,128)S(1)}) custom-call(s32[51]{0:T(128)S(1)} %get-tuple-element.863.source_ref, s32[51]{0:T(128)S(1)} %get-tuple-element.862.row_ref, s32[51]{0:T(128)S(1)} %get-tuple-element.708.lane_ref, f32[768,384]{1,0:T(8,128)} %get-tuple-element.1338.refs_0_, ...), custom_call_target="tpu_custom_call" | custom-call | bytes 15073280 | tf_op jit(solution)/shard_map/pallas_call | solution.py:79
  91.1 17.4 %shard_map.104 = (f32[512,6144]{1,0:T(8,128)}, f32[512,768]{1,0:T(8,128)}) custom-call(s32[1]{0:T(128)} %get-tuple-element.893.plane_ref, s32[6]{0:T(128)S(1)} %get-tuple-element.653.low_ref, s32[6]{0:T(128)S(1)} %get-tuple-element.652.high_ref, s32[6]{0:T(128)S(1)} %broadcast_in_dim.160.shift_ref, ...), custom_call_target="tpu_custom_call", output_to_operand_aliasing={{0}: (9, {}), {1}: (10, {})} | custom-call | flops 16106127360 | bytes 3932160 | tf_op jit(solution)/shard_map/pallas_call | solution.py:224
  108.5 5.0 collective-permute-done.37.refs_0_
  119.6 58.1 %collective-permute-done.41.refs_3_ = f32[16,128,128]{2,1,0:T(8,128)S(1)} collective-permute-done((f32[16,128,128]{2,1,0:T(8,128)}, f32[16,128,128]{2,1,0:T(8,128)S(1)}, u32[]{:S(2)}, u32[]{:S(2)}) %collective-permute-start.41) | collective-permute-done | bytes 1048608 | tf_op jit(solution)/shard_map/ppermute | solution.py:388
  198.3 15.1 %collective-permute-done.42.refs_2_.refs_0_ = f32[35,128,128]{2,1,0:T(8,128)} collective-permute-done((f32[35,128,128]{2,1,0:T(8,128)}, f32[35,128,128]{2,1,0:T(8,128)}, u32[]{:S(2)}, u32[]{:S(2)}) %collective-permute-start.42) | collective-permute-done | bytes 2293792 | tf_op jit(solution)/shard_map/ppermute | solution.py:388
  219.6 27.9 %shard_map.109 = (f32[512,6144]{1,0:T(8,128)}, f32[512,1536]{1,0:T(8,128)}) custom-call(s32[1]{0:T(128)} %get-tuple-element.893.plane_ref, s32[12]{0:T(128)S(1)} %pad_add_fusion.19.low_ref, s32[12]{0:T(128)S(1)} %pad_add_fusion.20.high_ref, s32[12]{0:T(128)S(1)} %concatenate.90.shift_ref, ...), custom_call_target="tpu_custom_call", output_to_operand_aliasing={{0}: (9, {}), {1}: (10, {})} | custom-call | flops 32212254720 | bytes 7864320 | tf_op jit(solution)/shard_map/pallas_call | solution.py:224
  248.7 16.2 %shard_map.110 = (f32[512,6144]{1,0:T(8,128)}, f32[512,768]{1,0:T(8,128)}) custom-call(s32[1]{0:T(128)} %get-tuple-element.893.plane_ref, s32[6]{0:T(128)S(1)} %get-tuple-element.649.low_ref, s32[6]{0:T(128)S(1)} %get-tuple-element.648.high_ref, s32[6]{0:T(128)S(1)} %broadcast_in_dim.162.shift_ref, ...), custom_call_target="tpu_custom_call", output_to_operand_aliasing={{0}: (9, {}), {1}: (10, {})} | custom-call | flops 16106127360 | bytes 3932160 | tf_op jit(solution)/shard_map/pallas_call | solution.py:224
  267.4 6.0 %collective-permute-start.51 = (f32[32,128,128]{2,1,0:T(8,128)}, f32[32,128,128]{2,1,0:T(8,128)}, u32[]{:S(2)}, u32[]{:S(2)}) collective-permute-start(f32[32,128,128]{2,1,0:T(8,128)} %collective-permute-done.46.refs_3_.refs_1_.refs_2_), channel_id=1, source_target_pairs={{0,2},{1,3},{2,6},{3,7},{6,4},{7,5},{4,0},{5,1},{8,10},{9,11},{10,... | collective-permute-start | bytes 6291464 | tf_op jit(solution)/shard_map/ppermute | solution.py:302
  273.4 14.9 %shard_map.112 = (f32[512,6144]{1,0:T(8,128)}, f32[512,768]{1,0:T(8,128)}) custom-call(s32[1]{0:T(128)} %get-tuple-element.892.plane_ref, s32[6]{0:T(128)S(1)} %get-tuple-element.651.low_ref, s32[6]{0:T(128)S(1)} %get-tuple-element.650.high_ref, s32[6]{0:T(128)S(1)} %broadcast_in_dim.161.shift_ref, ...), custom_call_target="tpu_custom_call", output_to_operand_aliasing={{0}: (9, {}), {1}: (10, {})} | custom-call | flops 16106127360 | bytes 3932160 | tf_op jit(solution)/shard_map/pallas_call | solution.py:224
  288.3 7.1 %collective-permute-done.43.refs_0_ = f32[35,128,128]{2,1,0:T(8,128)} collective-permute-done((f32[35,128,128]{2,1,0:T(8,128)}, f32[35,128,128]{2,1,0:T(8,128)}, u32[]{:S(2)}, u32[]{:S(2)}) %collective-permute-start.43) | collective-permute-done | bytes 2293792 | tf_op jit(solution)/shard_map/ppermute | solution.py:302
  302.6 25.0 %shard_map.114 = (f32[512,6144]{1,0:T(8,128)}, f32[512,1536]{1,0:T(8,128)}) custom-call(s32[1]{0:T(128)} %get-tuple-element.892.plane_ref, s32[12]{0:T(128)S(1)} %pad_add_fusion.21.low_ref, s32[12]{0:T(128)S(1)} %pad_add_fusion.22.high_ref, s32[12]{0:T(128)S(1)} %concatenate.93.shift_ref, ...), custom_call_target="tpu_custom_call", output_to_operand_aliasing={{0}: (9, {}), {1}: (10, {})} | custom-call | flops 32212254720 | bytes 7864320 | tf_op jit(solution)/shard_map/pallas_call | solution.py:224
  327.7 16.8 %shard_map.115 = (f32[512,6144]{1,0:T(8,128)}, f32[512,768]{1,0:T(8,128)}) custom-call(s32[1]{0:T(128)} %get-tuple-element.892.plane_ref, s32[6]{0:T(128)S(1)} %get-tuple-element.641.low_ref, s32[6]{0:T(128)S(1)} %get-tuple-element.640.high_ref, s32[6]{0:T(128)S(1)} %broadcast_in_dim.165.shift_ref, ...), custom_call_target="tpu_custom_call", output_to_operand_aliasing={{0}: (9, {}), {1}: (10, {})} | custom-call | flops 16106127360 | bytes 3932160 | tf_op jit(solution)/shard_map/pallas_call | solution.py:224
  344.5 4.5 collective-permute-done.49.refs_0_
  353.8 14.7 %shard_map.117 = (f32[512,6144]{1,0:T(8,128)}, f32[512,768]{1,0:T(8,128)}) custom-call(s32[1]{0:T(128)} %get-tuple-element.891.plane_ref, s32[6]{0:T(128)S(1)} %get-tuple-element.643.low_ref, s32[6]{0:T(128)S(1)} %get-tuple-element.642.high_ref, s32[6]{0:T(128)S(1)} %broadcast_in_dim.164.shift_ref, ...), custom_call_target="tpu_custom_call", output_to_operand_aliasing={{0}: (9, {}), {1}: (10, {})} | custom-call | flops 16106127360 | bytes 3932160 | tf_op jit(solution)/shard_map/pallas_call | solution.py:224
  368.6 20.9 %collective-permute-done.48.refs_0_ = f32[35,128,128]{2,1,0:T(8,128)} collective-permute-done((f32[35,128,128]{2,1,0:T(8,128)}, f32[35,128,128]{2,1,0:T(8,128)}, u32[]{:S(2)}, u32[]{:S(2)}) %collective-permute-start.48) | collective-permute-done | bytes 2293792 | tf_op jit(solution)/shard_map/ppermute | solution.py:302
  393.3 26.3 %shard_map.119 = (f32[512,6144]{1,0:T(8,128)}, f32[512,1536]{1,0:T(8,128)}) custom-call(s32[1]{0:T(128)} %get-tuple-element.891.plane_ref, s32[12]{0:T(128)S(1)} %pad_add_fusion.23.low_ref, s32[12]{0:T(128)S(1)} %pad_add_fusion.24.high_ref, s32[12]{0:T(128)S(1)} %concatenate.96.shift_ref, ...), custom_call_target="tpu_custom_call", output_to_operand_aliasing={{0}: (9, {}), {1}: (10, {})} | custom-call | flops 32212254720 | bytes 7864320 | tf_op jit(solution)/shard_map/pallas_call | solution.py:224
  419.7 19.6 %shard_map.120 = (f32[512,6144]{1,0:T(8,128)}, f32[512,768]{1,0:T(8,128)}) custom-call(s32[1]{0:T(128)} %get-tuple-element.891.plane_ref, s32[6]{0:T(128)S(1)} %get-tuple-element.635.low_ref, s32[6]{0:T(128)S(1)} %get-tuple-element.634.high_ref, s32[6]{0:T(128)S(1)} %broadcast_in_dim.167.shift_ref, ...), custom_call_target="tpu_custom_call", output_to_operand_aliasing={{0}: (9, {}), {1}: (10, {})} | custom-call | flops 16106127360 | bytes 3932160 | tf_op jit(solution)/shard_map/pallas_call | solution.py:224
  443.1 14.8 %shard_map.122 = (f32[512,6144]{1,0:T(8,128)}, f32[512,768]{1,0:T(8,128)}) custom-call(s32[1]{0:T(128)} %get-tuple-element.894.plane_ref, s32[6]{0:T(128)S(1)} %get-tuple-element.655.low_ref, s32[6]{0:T(128)S(1)} %get-tuple-element.654.high_ref, s32[6]{0:T(128)S(1)} %broadcast_in_dim.158.shift_ref, ...), custom_call_target="tpu_custom_call", output_to_operand_aliasing={{0}: (9, {}), {1}: (10, {})} | custom-call | flops 16106127360 | bytes 3932160 | tf_op jit(solution)/shard_map/pallas_call | solution.py:224
  462.7 28.0 %shard_map.123 = (f32[512,6144]{1,0:T(8,128)}, f32[512,1536]{1,0:T(8,128)}) custom-call(s32[1]{0:T(128)} %get-tuple-element.894.plane_ref, s32[12]{0:T(128)S(1)} %pad_add_fusion.17.low_ref, s32[12]{0:T(128)S(1)} %pad_add_fusion.18.high_ref, s32[12]{0:T(128)S(1)} %concatenate.87.shift_ref, ...), custom_call_target="tpu_custom_call", output_to_operand_aliasing={{0}: (9, {}), {1}: (10, {})} | custom-call | flops 32212254720 | bytes 7864320 | tf_op jit(solution)/shard_map/pallas_call | solution.py:224
  493.9 20.2 %shard_map.125 = (f32[512,6144]{1,0:T(8,128)}, f32[512,768]{1,0:T(8,128)}) custom-call(s32[1]{0:T(128)} %get-tuple-element.894.plane_ref, s32[6]{0:T(128)S(1)} %get-tuple-element.661.low_ref, s32[6]{0:T(128)S(1)} %get-tuple-element.660.high_ref, s32[6]{0:T(128)S(1)} %broadcast_in_dim.155.shift_ref, ...), custom_call_target="tpu_custom_call", output_to_operand_aliasing={{0}: (9, {}), {1}: (10, {})} | custom-call | flops 16106127360 | bytes 3932160 | tf_op jit(solution)/shard_map/pallas_call | solution.py:224
  514.5 4.8 shard_map.126.mine_in
  (317 shorter events, 92.2 us)
Async XLA Ops:
  15.3 36.0 %collective-permute-start.29 = (f32[768,384]{1,0:T(8,128)}, f32[768,384]{1,0:T(8,128)S(1)}, u32[]{:S(2)}, u32[]{:S(2)}) collective-permute-start(f32[768,384]{1,0:T(8,128)} %get-tuple-element.814.refs_1_), channel_id=1, source_target_pairs={{0,8},{8,0},{16,24},{24,16},{1,9},{9,1},{17,25},{25,17},{2,10},{10... | collective-permute-start | bytes 3538952 | tf_op jit(solution)/shard_map/ppermute | solution.py:296
  17.5 52.8 %collective-permute-start.30 = (f32[768,384]{1,0:T(8,128)}, f32[768,384]{1,0:T(8,128)S(1)}, u32[]{:S(2)}, u32[]{:S(2)}) collective-permute-start(f32[768,384]{1,0:T(8,128)} %get-tuple-element.813.refs_2_), channel_id=1, source_target_pairs={{0,16},{8,24},{16,0},{24,8},{1,17},{9,25},{17,1},{25,9},{2,18},{10... | collective-permute-start | bytes 3538952 | tf_op jit(solution)/shard_map/ppermute | solution.py:296
  19.2 51.1 %collective-permute-start.31 = (f32[768,384]{1,0:T(8,128)}, f32[768,384]{1,0:T(8,128)}, u32[]{:S(2)}, u32[]{:S(2)}) collective-permute-start(f32[768,384]{1,0:T(8,128)} %get-tuple-element.815.refs_3_), channel_id=1, source_target_pairs={{0,24},{8,16},{16,8},{24,0},{1,25},{9,17},{17,9},{25,1},{2,26},{10... | collective-permute-start | bytes 3538952 | tf_op jit(solution)/shard_map/ppermute | solution.py:296
  26.3 48.7 %collective-permute-start.32 = (f32[768,384]{1,0:T(8,128)}, f32[768,384]{1,0:T(8,128)}, u32[]{:S(2)}, u32[]{:S(2)}) collective-permute-start(f32[768,384]{1,0:T(8,128)} %get-tuple-element.1338.refs_0_), channel_id=1, source_target_pairs={{0,1},{1,0},{2,3},{3,2},{4,5},{5,4},{6,7},{7,6},{8,9},{9,8},{10,11... | collective-permute-start | bytes 3538952 | tf_op jit(solution)/shard_map/ppermute | solution.py:299
  114.8 67.4 %collective-permute-start.39 = (f32[35,128,128]{2,1,0:T(8,128)}, f32[35,128,128]{2,1,0:T(8,128)S(1)}, u32[]{:S(2)}, u32[]{:S(2)}) collective-permute-start(f32[35,128,128]{2,1,0:T(8,128)} %get-tuple-element.477), channel_id=1, source_target_pairs={{0,8},{1,17},{2,10},{3,19},{4,12},{5,21},{6,14},{7,23},{8,0},{9,25... | collective-permute-start | bytes 6881288 | tf_op jit(solution)/shard_map/ppermute | solution.py:388
  116.0 66.1 %collective-permute-start.40 = (f32[35,128,128]{2,1,0:T(8,128)}, f32[35,128,128]{2,1,0:T(8,128)S(1)}, u32[]{:S(2)}, u32[]{:S(2)}) collective-permute-start(f32[35,128,128]{2,1,0:T(8,128)} %get-tuple-element.477), channel_id=1, source_target_pairs={{0,16},{1,9},{2,18},{3,11},{4,20},{5,13},{6,22},{7,15},{8,24},{9,1... | collective-permute-start | bytes 6881288 | tf_op jit(solution)/shard_map/ppermute | solution.py:388
  117.1 60.7 %collective-permute-start.41 = (f32[16,128,128]{2,1,0:T(8,128)}, f32[16,128,128]{2,1,0:T(8,128)S(1)}, u32[]{:S(2)}, u32[]{:S(2)}) collective-permute-start(f32[16,128,128]{2,1,0:T(8,128)} %get-tuple-element.479.refs_1_), channel_id=1, source_target_pairs={{0,16},{1,9},{2,18},{3,11},{4,20},{5,13},{6,22},{7,15},{8,24},{9,1... | collective-permute-start | bytes 3145736 | tf_op jit(solution)/shard_map/ppermute | solution.py:388
  118.1 80.2 %collective-permute-start.36 = (f32[35,128,128]{2,1,0:T(8,128)}, f32[35,128,128]{2,1,0:T(8,128)}, u32[]{:S(2)}, u32[]{:S(2)}) collective-permute-start(f32[35,128,128]{2,1,0:T(8,128)} %copy-done.31), channel_id=1, source_target_pairs={{0,2},{1,3},{2,6},{3,7},{6,4},{7,5},{4,0},{5,1},{8,10},{9,11},{10,... | collective-permute-start | bytes 6881288 | tf_op jit(solution)/shard_map/ppermute | solution.py:302
  184.9 28.5 %collective-permute-start.42 = (f32[35,128,128]{2,1,0:T(8,128)}, f32[35,128,128]{2,1,0:T(8,128)}, u32[]{:S(2)}, u32[]{:S(2)}) collective-permute-start(f32[35,128,128]{2,1,0:T(8,128)} %get-tuple-element.481.refs_0_), channel_id=1, source_target_pairs={{0,16},{1,9},{2,18},{3,11},{4,20},{5,13},{6,22},{7,15},{8,24},{9,1... | collective-permute-start | bytes 6881288 | tf_op jit(solution)/shard_map/ppermute | solution.py:388
  196.6 68.3 %collective-permute-start.46 = (f32[32,128,128]{2,1,0:T(8,128)S(1)}, f32[32,128,128]{2,1,0:T(8,128)}, u32[]{:S(2)}, u32[]{:S(2)}) collective-permute-start(f32[32,128,128]{2,1,0:T(8,128)S(1)} %copy-done.14), channel_id=1, source_target_pairs={{0,2},{1,3},{2,6},{3,7},{6,4},{7,5},{4,0},{5,1},{8,10},{9,11},{10,... | collective-permute-start | bytes 6291464 | tf_op jit(solution)/shard_map/ppermute | solution.py:302
  213.4 52.5 %collective-permute-start.44 = (f32[35,128,128]{2,1,0:T(8,128)}, f32[35,128,128]{2,1,0:T(8,128)}, u32[]{:S(2)}, u32[]{:S(2)}) collective-permute-start(f32[35,128,128]{2,1,0:T(8,128)} %get-tuple-element.482.refs_0_), channel_id=1, source_target_pairs={{0,8},{1,17},{2,10},{3,19},{4,12},{5,21},{6,14},{7,23},{8,0},{9,25... | collective-permute-start | bytes 6881288 | tf_op jit(solution)/shard_map/ppermute | solution.py:388
  214.5 51.4 %collective-permute-start.45 = (f32[35,128,128]{2,1,0:T(8,128)}, f32[35,128,128]{2,1,0:T(8,128)}, u32[]{:S(2)}, u32[]{:S(2)}) collective-permute-start(f32[35,128,128]{2,1,0:T(8,128)} %get-tuple-element.482.refs_0_), channel_id=1, source_target_pairs={{0,16},{1,9},{2,18},{3,11},{4,20},{5,13},{6,22},{7,15},{8,24},{9,1... | collective-permute-start | bytes 6881288 | tf_op jit(solution)/shard_map/ppermute | solution.py:388
  215.6 79.8 %collective-permute-start.43 = (f32[35,128,128]{2,1,0:T(8,128)}, f32[35,128,128]{2,1,0:T(8,128)}, u32[]{:S(2)}, u32[]{:S(2)}) collective-permute-start(f32[35,128,128]{2,1,0:T(8,128)} %get-tuple-element.482.refs_0_), channel_id=1, source_target_pairs={{0,2},{1,3},{2,6},{3,7},{6,4},{7,5},{4,0},{5,1},{8,10},{9,11},{10,... | collective-permute-start | bytes 6881288 | tf_op jit(solution)/shard_map/ppermute | solution.py:302
  265.9 29.4 %collective-permute-start.47 = (f32[35,128,128]{2,1,0:T(8,128)}, f32[35,128,128]{2,1,0:T(8,128)S(1)}, u32[]{:S(2)}, u32[]{:S(2)}) collective-permute-start(f32[35,128,128]{2,1,0:T(8,128)} %get-tuple-element.489.refs_0_), channel_id=1, source_target_pairs={{0,16},{1,9},{2,18},{3,11},{4,20},{5,13},{6,22},{7,15},{8,24},{9,1... | collective-permute-start | bytes 6881288 | tf_op jit(solution)/shard_map/ppermute | solution.py:388
  267.4 77.0 %collective-permute-start.51 = (f32[32,128,128]{2,1,0:T(8,128)}, f32[32,128,128]{2,1,0:T(8,128)}, u32[]{:S(2)}, u32[]{:S(2)}) collective-permute-start(f32[32,128,128]{2,1,0:T(8,128)} %collective-permute-done.46.refs_3_.refs_1_.refs_2_), channel_id=1, source_target_pairs={{0,2},{1,3},{2,6},{3,7},{6,4},{7,5},{4,0},{5,1},{8,10},{9,11},{10,... | collective-permute-start | bytes 6291464 | tf_op jit(solution)/shard_map/ppermute | solution.py:302
  296.7 52.2 %collective-permute-start.49 = (f32[35,128,128]{2,1,0:T(8,128)}, f32[35,128,128]{2,1,0:T(8,128)S(1)}, u32[]{:S(2)}, u32[]{:S(2)}) collective-permute-start(f32[35,128,128]{2,1,0:T(8,128)} %get-tuple-element.490.refs_0_), channel_id=1, source_target_pairs={{0,8},{1,17},{2,10},{3,19},{4,12},{5,21},{6,14},{7,23},{8,0},{9,25... | collective-permute-start | bytes 6881288 | tf_op jit(solution)/shard_map/ppermute | solution.py:388
  298.3 50.7 %collective-permute-start.50 = (f32[35,128,128]{2,1,0:T(8,128)}, f32[35,128,128]{2,1,0:T(8,128)}, u32[]{:S(2)}, u32[]{:S(2)}) collective-permute-start(f32[35,128,128]{2,1,0:T(8,128)} %get-tuple-element.490.refs_0_), channel_id=1, source_target_pairs={{0,16},{1,9},{2,18},{3,11},{4,20},{5,13},{6,22},{7,15},{8,24},{9,1... | collective-permute-start | bytes 6881288 | tf_op jit(solution)/shard_map/ppermute | solution.py:388
  299.3 90.2 %collective-permute-start.48 = (f32[35,128,128]{2,1,0:T(8,128)}, f32[35,128,128]{2,1,0:T(8,128)}, u32[]{:S(2)}, u32[]{:S(2)}) collective-permute-start(f32[35,128,128]{2,1,0:T(8,128)} %get-tuple-element.490.refs_0_), channel_id=1, source_target_pairs={{0,2},{1,3},{2,6},{3,7},{6,4},{7,5},{4,0},{5,1},{8,10},{9,11},{10,... | collective-permute-start | bytes 6881288 | tf_op jit(solution)/shard_map/ppermute | solution.py:302
  350.4 39.0 %collective-permute-start.52 = (f32[35,128,128]{2,1,0:T(8,128)}, f32[35,128,128]{2,1,0:T(8,128)S(1)}, u32[]{:S(2)}, u32[]{:S(2)}) collective-permute-start(f32[35,128,128]{2,1,0:T(8,128)} %get-tuple-element.499.refs_0_), channel_id=1, source_target_pairs={{0,16},{1,9},{2,18},{3,11},{4,20},{5,13},{6,22},{7,15},{8,24},{9,1... | collective-permute-start | bytes 6881288 | tf_op jit(solution)/shard_map/ppermute | solution.py:388
  352.8 86.6 %collective-permute-start.55 = (f32[32,128,128]{2,1,0:T(8,128)}, f32[32,128,128]{2,1,0:T(8,128)}, u32[]{:S(2)}, u32[]{:S(2)}) collective-permute-start(f32[32,128,128]{2,1,0:T(8,128)} %collective-permute-done.51.refs_3_.refs_1_.refs_2_), channel_id=1, source_target_pairs={{0,2},{1,3},{2,6},{3,7},{6,4},{7,5},{4,0},{5,1},{8,10},{9,11},{10,... | collective-permute-start | bytes 6291464 | tf_op jit(solution)/shard_map/ppermute | solution.py:302
  390.8 52.3 %collective-permute-start.53 = (f32[35,128,128]{2,1,0:T(8,128)}, f32[35,128,128]{2,1,0:T(8,128)}, u32[]{:S(2)}, u32[]{:S(2)}) collective-permute-start(f32[35,128,128]{2,1,0:T(8,128)} %get-tuple-element.500.refs_0_), channel_id=1, source_target_pairs={{0,8},{1,17},{2,10},{3,19},{4,12},{5,21},{6,14},{7,23},{8,0},{9,25... | collective-permute-start | bytes 6881288 | tf_op jit(solution)/shard_map/ppermute | solution.py:388
  392.4 50.8 %collective-permute-start.54 = (f32[35,128,128]{2,1,0:T(8,128)}, f32[35,128,128]{2,1,0:T(8,128)}, u32[]{:S(2)}, u32[]{:S(2)}) collective-permute-start(f32[35,128,128]{2,1,0:T(8,128)} %get-tuple-element.500.refs_0_), channel_id=1, source_target_pairs={{0,16},{1,9},{2,18},{3,11},{4,20},{5,13},{6,22},{7,15},{8,24},{9,1... | collective-permute-start | bytes 6881288 | tf_op jit(solution)/shard_map/ppermute | solution.py:388
  457.9 33.0 %collective-permute-start.56 = (f32[512,768]{1,0:T(8,128)}, f32[512,768]{1,0:T(8,128)S(1)}, u32[]{:S(2)}, u32[]{:S(2)}) collective-permute-start(f32[512,768]{1,0:T(8,128)} %get-tuple-element.512), channel_id=1, source_target_pairs={{0,1},{1,0},{2,3},{3,2},{4,5},{5,4},{6,7},{7,6},{8,9},{9,8},{10,11... | collective-permute-start | bytes 4718600 | tf_op jit(solution)/shard_map/ppermute | solution.py:299
  459.4 34.4 %collective-permute-start.57 = (f32[35,128,128]{2,1,0:T(8,128)}, f32[35,128,128]{2,1,0:T(8,128)S(1)}, u32[]{:S(2)}, u32[]{:S(2)}) collective-permute-start(f32[35,128,128]{2,1,0:T(8,128)} %get-tuple-element.510.refs_0_), channel_id=1, source_target_pairs={{0,16},{1,9},{2,18},{3,11},{4,20},{5,13},{6,22},{7,15},{8,24},{9,1... | collective-permute-start | bytes 6881288 | tf_op jit(solution)/shard_map/ppermute | solution.py:388
  (62 other events, 781.8 us)
where the time goes:
time: 531 us; the launch traced here: 525 us
  Pallas kernels  289 us (54%)
  waiting for transfers between devices  136 us (26%)
  starting transfers between devices  45.1 us (8%)
  local copies, waits for them, and re-layouts  31.6 us (6%)
  between operations  12.9 us (2%)
  other arithmetic  9.55 us (2%)
    pallas_call x12, Pallas kernels, multiply(): pl.pallas_call(functools.partial(multiply_kernel, segments=segments, step...  242 us
    ppermute x15, waiting for transfers between devices, across(): lax.ppermute(x, ('row', 'col'), [(a * devices + d, (a ^ (near if d % CORE...  87.5 us
    ppermute x6, waiting for transfers between devices, by_plane(): lax.ppermute(x, 'col', [(ring[a] * CORES + c, ring[(a + 1) % Z] * CORES +...  27.9 us
    pallas_call x1, Pallas kernels, split_amplitudes(): pl.pallas_call(functools.partial(split_kernel, second=second, deep=deep),...  24.4 us
    ppermute x6, waiting for transfers between devices, by_row(): return lax.ppermute(x, 'row', [(a, a ^ distance) for a in range(R)])  19 us
    ppermute x15, starting transfers between devices, across(): lax.ppermute(x, ('row', 'col'), [(a * devices + d, (a ^ (near if d % CORE...  18.6 us
    ppermute x6, starting transfers between devices, by_plane(): lax.ppermute(x, 'col', [(ring[a] * CORES + c, ring[(a + 1) % Z] * CORES +...  15.5 us
    unnamed x101, local copies, waits for them, and re-layouts  13.6 us
  transfers between devices with their start and end apart: 36, of which 11 were waited for; matrix products, arithmetic and copies ran while one was open for 6% of the time, Pallas kernels for 50%

commit v1 on v0

--- a/solution.py
+++ b/solution.py
@@ -13,7 +13,8 @@
 VMEM_LIMIT = 48 * 1024 * 1024
 
 
-def split_kernel(mine_pattern, other_pattern, mine_ref, other_ref, out_ref, *cleared, second, deep):
+def split_kernel(mine_pattern, other_pattern, mine_ref, other_ref, lists_ref, out_ref, *cleared, second, deep):
+    del lists_ref
     rows = mine_ref.shape[0]
     for ref in cleared:
         ref[...] = jnp.zeros_like(ref)
@@ -30,7 +31,7 @@
                 out_ref[i, here, TILE:] = low
 
 
-def split_amplitudes(mine, other, mine_pattern, other_pattern, second, blocks):
+def split_amplitudes(mine, other, mine_pattern, other_pattern, lists, second, blocks):
     rows, depth = mine.shape
     tiles = depth // TILE
     deep = 4 if tiles % 4 == 0 else 1
@@ -45,26 +46,26 @@
         grid_spec=pltpu.PrefetchScalarGridSpec(
             num_scalar_prefetch=2,
             grid=(steps,),
-            in_specs=[pl.BlockSpec((rows, deep * TILE), lambda k, *_: (0, k))] * 2,
+            in_specs=[pl.BlockSpec((rows, deep * TILE), lambda k, *_: (0, k))] * 2 + [pl.BlockSpec(memory_space=pl.ANY)],
             out_specs=out_specs,
         ),
         out_shape=out_shape,
         compiler_params=pltpu.CompilerParams(vmem_limit_bytes=VMEM_LIMIT),
         cost_estimate=pl.CostEstimate(flops=8 * rows * depth, bytes_accessed=20 * rows * depth, transcendentals=0),
-    )(mine_pattern, other_pattern, mine, other)
+    )(mine_pattern, other_pattern, mine, other, lists)
     return made if len(made) == 2 else (made[0], jnp.zeros((rows, blocks * TILE), jnp.float32))
 
 
-def pack_kernel(source_ref, row_ref, lane_ref, *refs, plan, sources):
+def pack_kernel(lists_ref, *refs, plan, sources, at):
     ins, outs = refs[:sources], refs[sources:]
     for out, (base, size) in zip(outs, plan):
 
         def copy(slot, _, out=out, base=base):
-            row = pl.multiple_of(row_ref[base + slot], TILE)
-            lane = pl.multiple_of(lane_ref[base + slot], TILE)
+            row = pl.multiple_of(lists_ref[at["row"] + base + slot], TILE)
+            lane = pl.multiple_of(lists_ref[at["lane"] + base + slot], TILE)
             for source in range(sources):
 
-                @pl.when(source_ref[base + slot] == source)
+                @pl.when(lists_ref[at["source"] + base + slot] == source)
                 def _(source=source):
                     out[slot] = ins[source][pl.ds(row, TILE), pl.ds(lane, TILE)]
 
@@ -73,13 +74,13 @@
         lax.fori_loop(0, size, copy, 0)
 
 
-def pack(scalars, sources, plan):
+def pack(lists, at, sources, plan):
     whole = lambda x: pl.BlockSpec(x.shape, lambda g, *s: (0,) * len(x.shape))
     outs = [jax.ShapeDtypeStruct((size, TILE, TILE), jnp.float32) for _, size in plan]
     return pl.pallas_call(
-        functools.partial(pack_kernel, plan=plan, sources=len(sources)),
+        functools.partial(pack_kernel, plan=plan, sources=len(sources), at=at),
         grid_spec=pltpu.PrefetchScalarGridSpec(
-            num_scalar_prefetch=len(scalars),
+            num_scalar_prefetch=1,
             grid=(1,),
             in_specs=[whole(x) for x in sources],
             out_specs=[whole(x) for x in outs],
@@ -89,35 +90,35 @@
         cost_estimate=pl.CostEstimate(
             flops=0, bytes_accessed=4 * (sum(x.size for x in sources) + sum(x.size for x in outs)), transcendentals=0
         ),
-    )(*scalars, *sources)
-
-
-def pool_kernel(sizes_ref, offsets_ref, *refs):
+    )(lists, *sources)
+
+
+def pool_kernel(lists_ref, *refs, at):
     *ins, out = refs
     for e, ref in enumerate(ins):
 
         def copy(slot, _, ref=ref, e=e):
-            out[offsets_ref[e] + slot] = ref[slot]
+            out[lists_ref[at["offsets"] + e] + slot] = ref[slot]
             return 0
 
-        lax.fori_loop(0, sizes_ref[e], copy, 0)
-
-
-def pool(sizes, offsets, lists, capacity):
+        lax.fori_loop(0, lists_ref[at["sizes"] + e], copy, 0)
+
+
+def pool(lists, at, arrays, capacity):
     whole = lambda shape: pl.BlockSpec(shape, lambda g, *s: (0,) * len(shape))
     shape = (capacity, TILE, TILE)
     return pl.pallas_call(
-        pool_kernel,
+        functools.partial(pool_kernel, at=at),
         grid_spec=pltpu.PrefetchScalarGridSpec(
-            num_scalar_prefetch=2,
+            num_scalar_prefetch=1,
             grid=(1,),
-            in_specs=[whole(x.shape) for x in lists],
+            in_specs=[whole(x.shape) for x in arrays],
             out_specs=whole(shape),
         ),
         out_shape=jax.ShapeDtypeStruct(shape, jnp.float32),
         compiler_params=pltpu.CompilerParams(vmem_limit_bytes=VMEM_LIMIT),
         cost_estimate=pl.CostEstimate(flops=0, bytes_accessed=12 * capacity * TILE * TILE, transcendentals=0),
-    )(sizes, offsets, *lists)
+    )(lists, *arrays)
 
 
 def gate_kernel(*refs):
@@ -136,9 +137,17 @@
 
 
 def multiply_kernel(
-    plane_ref, low_ref, high_ref, shift_ref, base_ref, mine_at, other_at, kk_ref, amp_ref, mine_in, other_in, *refs,
-    segments, steps, per_chip, wide,
+    lists_ref, amp_ref, mine_in, other_in, *refs, at, turn, first, chips, segments, steps, per_chip, wide, long, straight
 ):
+    def spot(g):
+        column = g * wide
+        e = column // per_chip
+        return turn * chips + first + e, column - e * per_chip
+
+    def low_of(g, i):
+        listed, column = spot(g)
+        return lists_ref[at["bounds"] + listed * (per_chip + 1) + column + i]
+
     count = len(segments)
     tiles = refs[:count]
     mine_ref, other_ref, buffer, sem = refs[count:]
@@ -146,9 +155,9 @@
     rows = mine_ref.shape[0]
 
     def issue(g, half):
-        low, high = low_ref[g * wide], high_ref[g * wide + wide - 1]
+        low, high = low_of(g, 0), low_of(g, wide)
         for ref, (a, b, pooled, only) in zip(tiles, segments):
-            shift = shift_ref[g * wide] if pooled else -a
+            shift = lists_ref[at["offsets"] + spot(g)[0]] - straight if pooled else -a
 
             def start(slot, _, ref=ref, shift=shift):
                 pltpu.make_async_copy(
@@ -174,16 +183,16 @@
 
     mine_ref[...] = mine_in[...]
     other_ref[...] = other_in[...]
-    origin = low_ref[step * wide]
+    origin = low_of(step, 0)
     for i in range(wide):
         lanes = pl.ds(i * TILE, TILE)
-        low = low_ref[step * wide + i]
-        length = high_ref[step * wide + i] - low
-        base = base_ref[step * wide] + low
-
-        def wait(at, _, low=low):
-            at = low - origin + at
-            pltpu.make_async_copy(tiles[0].at[0], buffer.at[half, at], sem.at[half, at]).wait()
+        low = low_of(step, i)
+        length = low_of(step, i + 1) - low
+        base = at["kk"] + spot(step)[0] * long + low
+
+        def wait(place, _, low=low):
+            place = low - origin + place
+            pltpu.make_async_copy(tiles[0].at[0], buffer.at[half, place], sem.at[half, place]).wait()
             return 0
 
         lax.fori_loop(0, length, wait, 0)
@@ -191,17 +200,17 @@
         def add(turn, _, lanes=lanes, low=low, length=length, base=base):
             weights, ks = [], []
             for u in range(UNROLL):
-                at = turn * UNROLL + u
-                inside = at < length
-                at = jnp.minimum(at, length - 1)
-                value = buffer[half, low - origin + at]
+                place = turn * UNROLL + u
+                inside = place < length
+                place = jnp.minimum(place, length - 1)
+                value = buffer[half, low - origin + place]
                 if u:
                     value = jnp.where(inside, value, 0.0)
                 high = value.astype(jnp.bfloat16)
                 rest = (value - high.astype(jnp.float32)).astype(jnp.bfloat16)
                 weights.append(jnp.concatenate([high, rest], axis=1))
                 weights.append(jnp.concatenate([high, jnp.zeros_like(high)], axis=1))
-                ks.append(kk_ref[base + at])
+                ks.append(lists_ref[base + place])
             left = jnp.concatenate([amp_ref[k] for k in ks], axis=1)
             product = jnp.dot(left, jnp.concatenate(weights, axis=0), preferred_element_type=jnp.float32)
             total = product[:, :TILE] + product[:, TILE:]
@@ -212,22 +221,36 @@
         lax.fori_loop(0, (length + UNROLL - 1) // UNROLL, add, 0)
 
 
-def multiply(scalars, steps, per_chip, wide, amps, mine, other, pieces, kd):
+def multiply(lists, at, turn, first, count, chips, per_chip, wide, long, straight, amps, mine, other, pieces, kd, spot):
     rows = mine.shape[0]
     segments = [piece[1:] for piece in pieces]
+    blocks = per_chip // wide
+    steps = count * blocks
     expected = 10 * steps * wide
-    n = len(scalars)
-    mine_spec = pl.BlockSpec((rows, wide * TILE), lambda g, *s: (0, s[5][g]))
-    other_spec = pl.BlockSpec((rows, wide * TILE), lambda g, *s: (0, s[6][g]))
+    n = 1
+    mine_spec = pl.BlockSpec((rows, wide * TILE), lambda g, s: (0, s[at["mine"] + first * blocks + g]))
+    other_spec = pl.BlockSpec((rows, wide * TILE), lambda g, s: (0, spot * blocks + g))
     anywhere = pl.BlockSpec(memory_space=pl.ANY)
     held = CORES * kd * wide
     return pl.pallas_call(
-        functools.partial(multiply_kernel, segments=segments, steps=steps, per_chip=per_chip, wide=wide),
+        functools.partial(
+            multiply_kernel,
+            at=at,
+            turn=turn,
+            first=first,
+            chips=chips,
+            segments=segments,
+            steps=steps,
+            per_chip=per_chip,
+            wide=wide,
+            long=long,
+            straight=straight,
+        ),
         grid_spec=pltpu.PrefetchScalarGridSpec(
             num_scalar_prefetch=n,
             grid=(steps,),
             in_specs=[
-                pl.BlockSpec((CORES * kd, CORES * rows, 2 * TILE), lambda g, *s: (s[0][0], 0, 0)),
+                pl.BlockSpec((CORES * kd, CORES * rows, 2 * TILE), lambda g, s: (s[at["planes"] + turn], 0, 0)),
                 mine_spec,
                 other_spec,
             ]
@@ -243,7 +266,7 @@
             bytes_accessed=expected * 4 * TILE * TILE,
             transcendentals=0,
         ),
-    )(*scalars, amps, mine, other, *[piece[0] for piece in pieces])
+    )(lists, amps, mine, other, *[piece[0] for piece in pieces])
 
 
 def place_kernel(at_ref, mine_in, piece_ref, out_ref):
@@ -314,14 +337,6 @@
         (int_pattern,) = gate([int_pattern], shares[1:])
     for d in range(1, groups):
         shares[d] = by_row(shares[d], d)
-
-    amps_mine = amplitudes.reshape(rows, depth)
-    amps, mine = split_amplitudes(
-        amps_mine, by_core(amps_mine), amp_pattern, by_core(amp_pattern), second, blocks + spare
-    )
-    if groups > 1:
-        shares[1:] = gate(shares[1:], [amps])
-    twins = [by_core(x) for x in shares]
 
     patterns = [int_pattern] + [by_row(int_pattern, d) for d in range(1, R)]
     by_distance = jnp.stack(patterns).reshape(R, Z, CORES * kd, groups, width)
@@ -362,9 +377,9 @@
     )
     ends = jnp.sum(own[:, :, None, :] * (ids[None, :] < (jnp.arange(per_chip + 1) * CORES * kd)[:, None]), axis=-1)
 
-    straight = max(2, round(tiles * 35 / 72)) if R == 4 else max(4, 2 * round(tiles * 25 / 72))
-    extra = max(2, round(tiles * 16 / 72)) if R == 4 else 0
-    pooled = max(R, round(tiles * 32 / 72)) if R == 4 else 0
+    straight = max(2, round(tiles * 38 / 72)) if R == 4 else max(4, 2 * round(tiles * 25 / 72))
+    extra = max(2, round(tiles * 12 / 72)) if R == 4 else 0
+    pooled = max(R, round(tiles * 20 / 72)) if R == 4 else 0
     longest = tiles + straight + extra
     slots = jnp.pad(slots, ((0, 0), (0, 0), (0, longest - tiles)), constant_values=-1)
     most = jnp.max(cores_counts)
@@ -395,44 +410,72 @@
             ],
         )
 
-    def one_round(state, others):
-        base, mine = state
-        others = list(others)
+    def listed(base):
         after = base + straight
         left = jnp.clip(cores_counts - after, 0, extra)
         fits = jnp.max(jnp.sum(left, axis=1)) <= pooled
         taken = jnp.where(fits, extra, pooled // R) if extra else jnp.int32(0)
         sizes = jnp.clip(counts - after, 0, taken)
         before = chip_of[None, :] < chip_of[:, None]
-        offsets = jnp.sum(sizes[:, None, :] * before[None], axis=-1).astype(jnp.int32)
+        offsets = jnp.sum(sizes[:, None, :] * before[None], axis=-1)
         now = lax.dynamic_slice_in_dim(slots, base, straight + extra, axis=2)
         kk = jnp.maximum(now, 0) % (CORES * kd)
-        bounds = jnp.clip(ends - base, 0, straight + taken).astype(jnp.int32)
-
+        bounds = jnp.clip(ends - base, 0, straight + taken)
         column = jnp.asarray(owned)[core][jnp.maximum(now[0, 0], 0) // (CORES * kd)]
         holder = kk[0, 0] // kd
         source = jnp.where(now[0, 0] < 0, -1, (holder != core) * groups + column // width)
-        where = [source, kk[0, 0] % kd * TILE, column % width * TILE]
+        found = {
+            "source": source,
+            "row": kk[0, 0] % kd * TILE,
+            "lane": column % width * TILE,
+            "sizes": sizes,
+            "offsets": offsets,
+            "bounds": bounds,
+            "kk": kk,
+            "mine": mine_at,
+            "planes": planes,
+        }
+        at, total = {}, 0
+        for name, x in found.items():
+            at[name] = total
+            total += x.size
+        return jnp.concatenate([x.reshape(-1).astype(jnp.int32) for x in found.values()]), at, taken
+
+    first_lists = listed(jnp.int32(0))
+    amps_mine = amplitudes.reshape(rows, depth)
+    amps, mine = split_amplitudes(
+        amps_mine, by_core(amps_mine), amp_pattern, by_core(amp_pattern), first_lists[0], second, blocks + spare
+    )
+    if groups > 1:
+        shares[1:] = gate(shares[1:], [amps])
+    twins = [by_core(x) for x in shares]
+
+    def one_round(state, others, made):
+        base, mine = state
+        others = list(others)
+        lists, at, taken = made
         plan = ((0, straight), (straight, extra), (0, straight)) if extra else ((0, straight),)
-        packed = pack([x.astype(jnp.int32) for x in where], shares + twins, plan)
-
-
-        def add(mine, other, step, neighbours, low_slot, high_slot, pieces, spot=0):
-            low, high, shift, base_at = [], [], [], []
-            for e in neighbours:
-                limits = jnp.clip(bounds[step, e], low_slot, high_slot)
-                low.append(limits[:-1])
-                high.append(limits[1:])
-                shift.append(jnp.broadcast_to(offsets[step, e] - straight, (per_chip,)))
-                base_at.append(jnp.full((per_chip,), (e - neighbours[0]) * (straight + extra)))
-            first_e, last_e = neighbours[0], neighbours[-1] + 1
-            lists = [jnp.concatenate(x) for x in (low, high, shift, base_at)]
-            lists.append(mine_at[first_e:last_e].reshape(-1))
-            steps = len(neighbours) * per_chip // wide
-            lists.append(jnp.arange(steps) + spot * per_chip // wide)
-            scalars = [planes[step].reshape(1), *lists, kk[step, first_e:last_e].reshape(-1)]
-            scalars = [x.astype(jnp.int32) for x in scalars]
-            return multiply(scalars, steps, per_chip, wide, amps, mine, other, pieces, kd)
+        packed = pack(lists, at, shares + twins, plan)
+
+        def add(mine, other, step, neighbours, pieces, spot=0):
+            return multiply(
+                lists,
+                at,
+                step,
+                neighbours[0],
+                len(neighbours),
+                R,
+                per_chip,
+                wide,
+                straight + extra,
+                straight,
+                amps,
+                mine,
+                other,
+                pieces,
+                kd,
+                spot,
+            )
 
         if R == 4:
             end = straight + extra
@@ -440,14 +483,14 @@
             along = [sent, by_plane(sent)]
             first_late, second_late = across(late, 1), across(late, 2)
             at_home = [(sent, 0, straight, False, None), (late, straight, end, False, None)]
-            mine, others[0] = add(mine, others[0], 0, [0], 0, end, at_home)
+            mine, others[0] = add(mine, others[0], 0, [0], at_home)
             first_late, ready, mine = gate([first_late, ready, mine], [second_late])
             third_late = across(first_late, 2)
             first_near, second_near = across(ready, 1), across(ready, 2)
             pools = [
                 pool(
-                    sizes[0].astype(jnp.int32),
-                    offsets[0],
+                    lists,
+                    at,
                     [late, first_late, second_late, third_late],
                     pooled,
                 )
@@ -462,7 +505,7 @@
                 last = [(third_near, 0, straight, False, None), mixed]
                 if step:
                     home = [(along[step], 0, straight, False, None), mixed]
-                    mine, others[0] = add(mine, others[0], step, [0], 0, end, home)
+                    mine, others[0] = add(mine, others[0], step, [0], home)
                 if step == Z - 1:
                     received.append(by_core(others[0]))
                 else:
@@ -471,11 +514,11 @@
                     if step + 2 < Z:
                         along.append(by_plane(along[step + 1]))
                         pools.append(by_plane(pools[step + 1]))
-                mine, others[1] = add(mine, others[1], step, [1, 2], 0, end, near)
+                mine, others[1] = add(mine, others[1], step, [1, 2], near)
                 if step == Z - 1:
                     received.append(by_core(others[1]))
                     mine = place(received_at[0], wide, mine, received[0])
-                mine, others[2] = add(mine, others[2], step, [3], 0, end, last)
+                mine, others[2] = add(mine, others[2], step, [3], last)
             received.append(by_core(others[2]))
             mine = place(received_at[1:3].reshape(-1), wide, mine, received[1])
             mine = place(received_at[3], wide, mine, received[2])
@@ -484,17 +527,17 @@
             for step in range(Z):
                 for e in range(R):
                     piece = by_row(now_at, e) if e else now_at
-                    mine, others[0] = add(mine, others[0], step, [e], 0, straight, [(piece, 0, straight, False, None)], e)
+                    mine, others[0] = add(mine, others[0], step, [e], [(piece, 0, straight, False, None)], e)
                 if step + 1 < Z:
                     now_at = by_plane(now_at)
             mine = place(received_at.reshape(-1), wide, mine, by_core(others[0]))
         return base + straight + taken, mine
 
-    state = one_round((jnp.int32(0), mine), others)
+    state = one_round((jnp.int32(0), mine), others, first_lists)
     cleared = [x.shape for x in others]
     _, mine = lax.while_loop(
         lambda state: state[0] < most,
-        lambda state: one_round(state, [jnp.zeros(shape, jnp.float32) for shape in cleared]),
+        lambda state: one_round(state, [jnp.zeros(shape, jnp.float32) for shape in cleared], listed(state[0])),
         state,
     )
     return mine[:, : blocks * TILE].reshape(first, second, blocks * TILE)

time: 531 us -> 531 us (level)
  waiting for transfers between devices: 136 us -> 154 us
  starting transfers between devices: 45.1 us -> 33.8 us
  between operations: 12.9 us -> 2.71 us
    ppermute x15, waiting for transfers between devices: 87.5 us -> 132 us  [across(): lax.ppermute(x, ('row', 'col'), [(a * devices + d, (a ^ (near if d % CORE...]
    ppermute x6, waiting for transfers between devices: 27.9 us -> 0.02 us  [by_plane(): lax.ppermute(x, 'col', [(ring[a] * CORES + c, ring[(a + 1) % Z] * CORES +...]
    ppermute x6, starting transfers between devices: 15.5 us -> 6.71 us  [by_plane(): lax.ppermute(x, 'col', [(ring[a] * CORES + c, ring[(a + 1) % Z] * CORES +...]
    unnamed x101 -> x107, local copies, waits for them, and re-layouts: 13.6 us -> 19.3 us
  transfers between devices with their start and end apart: 36 -> 36, of which waited for: 11 -> 13; matrix products, arithmetic and copies ran while one was open for 6% -> 5% of each run, Pallas kernels for 50% -> 50%
where the time goes in v1:
time: 531 us; the launch traced here: 522 us
  Pallas kernels  287 us (54%)
  waiting for transfers between devices  154 us (29%)
  local copies, waits for them, and re-layouts  34.5 us (6%)
  starting transfers between devices  33.8 us (6%)
  other arithmetic  8.24 us (2%)
    pallas_call x12, Pallas kernels, multiply(): pl.pallas_call(functools.partial(multiply_kernel, at=at, turn=turn, first...  241 us
    ppermute x15, waiting for transfers between devices, across(): lax.ppermute(x, ('row', 'col'), [(a * devices + d, (a ^ (near if d % CORE...  132 us
    pallas_call x1, Pallas kernels, split_amplitudes(): pl.pallas_call(functools.partial(split_kernel, second=second, deep=deep),...  24.3 us
    unnamed x107, local copies, waits for them, and re-layouts  19.3 us
    ppermute x6, waiting for transfers between devices, by_row(): return lax.ppermute(x, 'row', [(a, a ^ distance) for a in range(R)])  16.1 us
    ppermute x15, starting transfers between devices, across(): lax.ppermute(x, ('row', 'col'), [(a * devices + d, (a ^ (near if d % CORE...  16.1 us
    pallas_call x3, Pallas kernels, place(): pl.pallas_call(place_kernel, grid_spec=pltpu.PrefetchScalarGridSpec(num_s...  11.1 us
  transfers between devices with their start and end apart: 36, of which 13 were waited for; matrix products, arithmetic and copies ran while one was open for 5% of the time, Pallas kernels for 50%

profile of v1, /device:TPU:0, one launch (start us, length us, event | category | flops | bytes accessed | tf_op | source)
XLA Modules:
  0.0 521.8 jit_solution(4895318185093804067)
XLA Ops:
  1.8 4.6 fusion.28
  30.3 24.3 %shard_map.101 = (bf16[48,1024,256]{2,1,0:T(8,128)(2,1)}, f32[512,6144]{1,0:T(8,128)}) custom-call(s32[16,48]{1,0:T(8,128)S(1)} %copy-done.38, s32[16,48]{1,0:T(8,128)S(1)} %collective-permute-done.27.other_pattern, f32[512,6144]{1,0:T(8,128)} %bitcast.176, f32[512,6144]{1,0:T(8,128)} %collective-permute-done.28.other_ref, s32[1106]{0:T(1024)S(1)} %concatenate.19.lists_ref), custom_call_target="tpu_custom_call" | custom-call | flops 25165824 | bytes 62914560 | tf_op jit(solution)/shard_map/pallas_call | solution.py:44
  54.7 16.1 %collective-permute-done.30.refs_1_ = f32[768,384]{1,0:T(8,128)S(1)} collective-permute-done((f32[768,384]{1,0:T(8,128)}, f32[768,384]{1,0:T(8,128)S(1)}, u32[]{:S(2)}, u32[]{:S(2)}) %collective-permute-start.30) | collective-permute-done | bytes 1179680 | tf_op jit(solution)/shard_map/ppermute | solution.py:319
  77.3 9.7 %shard_map.103 = (f32[38,128,128]{2,1,0:T(8,128)S(1)}, f32[12,128,128]{2,1,0:T(8,128)S(1)}, f32[38,128,128]{2,1,0:T(8,128)S(1)}) custom-call(s32[1106]{0:T(1024)S(1)} %concatenate.19.lists_ref, f32[768,384]{1,0:T(8,128)} %get-tuple-element.1173.refs_0_, f32[768,384]{1,0:T(8,128)S(1)} %get-tuple-element.1174.refs_1_, f32[768,384]{1,0:T(8,128)} %copy-done.46, ...), custom_call_target="tpu_custom_call" | custom-call | bytes 15204352 | tf_op jit(solution)/shard_map/pallas_call | solution.py:80
  91.8 17.5 %shard_map.104 = (f32[512,6144]{1,0:T(8,128)}, f32[512,768]{1,0:T(8,128)}) custom-call(s32[1106]{0:T(1024)S(1)} %concatenate.19.lists_ref, bf16[48,1024,256]{2,1,0:T(8,128)(2,1)} %get-tuple-element.1181.refs_3_.amp_ref, f32[512,6144]{1,0:T(8,128)} %get-tuple-element.455.mine_in, ...), custom_call_target="tpu_custom_call", output_to_operand_aliasing={{0}: (2, {}), {1}: (3, {})} | custom-call | flops 16106127360 | bytes 3932160 | tf_op jit(solution)/shard_map/pallas_call | solution.py:235
  110.5 3.9 collective-permute-start.39
  116.4 60.3 %collective-permute-done.41.refs_3_ = f32[12,128,128]{2,1,0:T(8,128)S(1)} collective-permute-done((f32[12,128,128]{2,1,0:T(8,128)}, f32[12,128,128]{2,1,0:T(8,128)S(1)}, u32[]{:S(2)}, u32[]{:S(2)}) %collective-permute-start.41) | collective-permute-done | bytes 786464 | tf_op jit(solution)/shard_map/ppermute | solution.py:403
  186.5 27.8 %collective-permute-done.42.refs_2_.refs_0_ = f32[38,128,128]{2,1,0:T(8,128)} collective-permute-done((f32[38,128,128]{2,1,0:T(8,128)}, f32[38,128,128]{2,1,0:T(8,128)}, u32[]{:S(2)}, u32[]{:S(2)}) %collective-permute-start.42) | collective-permute-done | bytes 2490400 | tf_op jit(solution)/shard_map/ppermute | solution.py:403
  219.4 31.4 %shard_map.109 = (f32[512,6144]{1,0:T(8,128)}, f32[512,1536]{1,0:T(8,128)}) custom-call(s32[1106]{0:T(1024)S(1)} %concatenate.19.lists_ref, bf16[48,1024,256]{2,1,0:T(8,128)(2,1)} %get-tuple-element.1181.refs_3_.amp_ref, f32[512,6144]{1,0:T(8,128)} %get-tuple-element.463.mine_in, ...), custom_call_target="tpu_custom_call", output_to_operand_aliasing={{0}: (2, {}), {1}: (3, {})} | custom-call | flops 32212254720 | bytes 7864320 | tf_op jit(solution)/shard_map/pallas_call | solution.py:235
  252.1 15.5 %shard_map.110 = (f32[512,6144]{1,0:T(8,128)}, f32[512,768]{1,0:T(8,128)}) custom-call(s32[1106]{0:T(1024)S(1)} %concatenate.19.lists_ref, bf16[48,1024,256]{2,1,0:T(8,128)(2,1)} %get-tuple-element.1181.refs_3_.amp_ref, f32[512,6144]{1,0:T(8,128)} %get-tuple-element.464.mine_in, ...), custom_call_target="tpu_custom_call", output_to_operand_aliasing={{0}: (2, {}), {1}: (3, {})} | custom-call | flops 16106127360 | bytes 3932160 | tf_op jit(solution)/shard_map/pallas_call | solution.py:235
  274.0 14.1 %shard_map.112 = (f32[512,6144]{1,0:T(8,128)}, f32[512,768]{1,0:T(8,128)}) custom-call(s32[1106]{0:T(1024)S(1)} %concatenate.19.lists_ref, bf16[48,1024,256]{2,1,0:T(8,128)(2,1)} %get-tuple-element.1181.refs_3_.amp_ref, f32[512,6144]{1,0:T(8,128)} %get-tuple-element.466.mine_in, ...), custom_call_target="tpu_custom_call", output_to_operand_aliasing={{0}: (2, {}), {1}: (3, {})} | custom-call | flops 16106127360 | bytes 3932160 | tf_op jit(solution)/shard_map/pallas_call | solution.py:235
  288.1 13.3 %collective-permute-done.47.refs_2_.refs_0_ = f32[38,128,128]{2,1,0:T(8,128)S(1)} collective-permute-done((f32[38,128,128]{2,1,0:T(8,128)}, f32[38,128,128]{2,1,0:T(8,128)S(1)}, u32[]{:S(2)}, u32[]{:S(2)}) %collective-permute-start.47) | collective-permute-done | bytes 2490400 | tf_op jit(solution)/shard_map/ppermute | solution.py:403
  306.9 24.4 %shard_map.114 = (f32[512,6144]{1,0:T(8,128)}, f32[512,1536]{1,0:T(8,128)}) custom-call(s32[1106]{0:T(1024)S(1)} %concatenate.19.lists_ref, bf16[48,1024,256]{2,1,0:T(8,128)(2,1)} %get-tuple-element.1181.refs_3_.amp_ref, f32[512,6144]{1,0:T(8,128)} %get-tuple-element.471.mine_in, ...), custom_call_target="tpu_custom_call", output_to_operand_aliasing={{0}: (2, {}), {1}: (3, {})} | custom-call | flops 32212254720 | bytes 7864320 | tf_op jit(solution)/shard_map/pallas_call | solution.py:235
  331.3 18.8 %shard_map.115 = (f32[512,6144]{1,0:T(8,128)}, f32[512,768]{1,0:T(8,128)}) custom-call(s32[1106]{0:T(1024)S(1)} %concatenate.19.lists_ref, bf16[48,1024,256]{2,1,0:T(8,128)(2,1)} %get-tuple-element.1181.refs_3_.amp_ref, f32[512,6144]{1,0:T(8,128)} %get-tuple-element.473.mine_in, ...), custom_call_target="tpu_custom_call", output_to_operand_aliasing={{0}: (2, {}), {1}: (3, {})} | custom-call | flops 16106127360 | bytes 3932160 | tf_op jit(solution)/shard_map/pallas_call | solution.py:235
  350.1 8.3 %collective-permute-done.49.refs_0_ = f32[38,128,128]{2,1,0:T(8,128)S(1)} collective-permute-done((f32[38,128,128]{2,1,0:T(8,128)}, f32[38,128,128]{2,1,0:T(8,128)S(1)}, u32[]{:S(2)}, u32[]{:S(2)}) %collective-permute-start.49) | collective-permute-done | bytes 2490400 | tf_op jit(solution)/shard_map/ppermute | solution.py:403
  362.8 14.1 %shard_map.117 = (f32[512,6144]{1,0:T(8,128)}, f32[512,768]{1,0:T(8,128)}) custom-call(s32[1106]{0:T(1024)S(1)} %concatenate.19.lists_ref, bf16[48,1024,256]{2,1,0:T(8,128)(2,1)} %get-tuple-element.1181.refs_3_.amp_ref, f32[512,6144]{1,0:T(8,128)} %get-tuple-element.476.mine_in, ...), custom_call_target="tpu_custom_call", output_to_operand_aliasing={{0}: (2, {}), {1}: (3, {})} | custom-call | flops 16106127360 | bytes 3932160 | tf_op jit(solution)/shard_map/pallas_call | solution.py:235
  376.9 13.4 %collective-permute-done.52.refs_2_.refs_0_ = f32[38,128,128]{2,1,0:T(8,128)S(1)} collective-permute-done((f32[38,128,128]{2,1,0:T(8,128)}, f32[38,128,128]{2,1,0:T(8,128)S(1)}, u32[]{:S(2)}, u32[]{:S(2)}) %collective-permute-start.52) | collective-permute-done | bytes 2490400 | tf_op jit(solution)/shard_map/ppermute | solution.py:403
  393.4 30.0 %shard_map.119 = (f32[512,6144]{1,0:T(8,128)}, f32[512,1536]{1,0:T(8,128)}) custom-call(s32[1106]{0:T(1024)S(1)} %concatenate.19.lists_ref, bf16[48,1024,256]{2,1,0:T(8,128)(2,1)} %get-tuple-element.1181.refs_3_.amp_ref, f32[512,6144]{1,0:T(8,128)} %get-tuple-element.481.mine_in, ...), custom_call_target="tpu_custom_call", output_to_operand_aliasing={{0}: (2, {}), {1}: (3, {})} | custom-call | flops 32212254720 | bytes 7864320 | tf_op jit(solution)/shard_map/pallas_call | solution.py:235
  423.5 17.2 %shard_map.120 = (f32[512,6144]{1,0:T(8,128)}, f32[512,768]{1,0:T(8,128)}) custom-call(s32[1106]{0:T(1024)S(1)} %concatenate.19.lists_ref, bf16[48,1024,256]{2,1,0:T(8,128)(2,1)} %get-tuple-element.1181.refs_3_.amp_ref, f32[512,6144]{1,0:T(8,128)} %get-tuple-element.483.mine_in, ...), custom_call_target="tpu_custom_call", output_to_operand_aliasing={{0}: (2, {}), {1}: (3, {})} | custom-call | flops 16106127360 | bytes 3932160 | tf_op jit(solution)/shard_map/pallas_call | solution.py:235
  440.7 4.9 collective-permute-done.53.refs_0_
  445.6 14.8 %shard_map.122 = (f32[512,6144]{1,0:T(8,128)}, f32[512,768]{1,0:T(8,128)}) custom-call(s32[1106]{0:T(1024)S(1)} %concatenate.19.lists_ref, bf16[48,1024,256]{2,1,0:T(8,128)(2,1)} %get-tuple-element.1181.refs_3_.amp_ref, f32[512,6144]{1,0:T(8,128)} %get-tuple-element.486.mine_in, ...), custom_call_target="tpu_custom_call", output_to_operand_aliasing={{0}: (2, {}), {1}: (3, {})} | custom-call | flops 16106127360 | bytes 3932160 | tf_op jit(solution)/shard_map/pallas_call | solution.py:235
  461.9 24.1 %shard_map.123 = (f32[512,6144]{1,0:T(8,128)}, f32[512,1536]{1,0:T(8,128)}) custom-call(s32[1106]{0:T(1024)S(1)} %concatenate.19.lists_ref, bf16[48,1024,256]{2,1,0:T(8,128)(2,1)} %get-tuple-element.1181.refs_3_.amp_ref, f32[512,6144]{1,0:T(8,128)} %get-tuple-element.488.mine_in, ...), custom_call_target="tpu_custom_call", output_to_operand_aliasing={{0}: (2, {}), {1}: (3, {})} | custom-call | flops 32212254720 | bytes 7864320 | tf_op jit(solution)/shard_map/pallas_call | solution.py:235
  491.0 19.3 %shard_map.125 = (f32[512,6144]{1,0:T(8,128)}, f32[512,768]{1,0:T(8,128)}) custom-call(s32[1106]{0:T(1024)S(1)} %concatenate.19.lists_ref, bf16[48,1024,256]{2,1,0:T(8,128)(2,1)} %get-tuple-element.1181.refs_3_.amp_ref, f32[512,6144]{1,0:T(8,128)} %shard_map.124.mine_in, ...), custom_call_target="tpu_custom_call", output_to_operand_aliasing={{0}: (2, {}), {1}: (3, {})} | custom-call | flops 16106127360 | bytes 3932160 | tf_op jit(solution)/shard_map/pallas_call | solution.py:235
  510.8 4.8 shard_map.126.mine_in
  (269 shorter events, 86.5 us)
Async XLA Ops:
  0.0 30.3 %collective-permute-start.28 = (f32[512,6144]{1,0:T(8,128)}, f32[512,6144]{1,0:T(8,128)}, u32[]{:S(2)}, u32[]{:S(2)}) collective-permute-start(f32[512,6144]{1,0:T(8,128)} %bitcast.175), channel_id=1, source_target_pairs={{0,1},{1,0},{2,3},{3,2},{4,5},{5,4},{6,7},{7,6},{8,9},{9,8},{10,11... | collective-permute-start | bytes 37748744 | tf_op jit(solution)/shard_map/ppermute | solution.py:322
  15.8 38.8 %collective-permute-start.29 = (f32[768,384]{1,0:T(8,128)}, f32[768,384]{1,0:T(8,128)S(1)}, u32[]{:S(2)}, u32[]{:S(2)}) collective-permute-start(f32[768,384]{1,0:T(8,128)} %get-tuple-element.858.refs_1_), channel_id=1, source_target_pairs={{0,8},{8,0},{16,24},{24,16},{1,9},{9,1},{17,25},{25,17},{2,10},{10... | collective-permute-start | bytes 3538952 | tf_op jit(solution)/shard_map/ppermute | solution.py:319
  18.0 52.8 %collective-permute-start.30 = (f32[768,384]{1,0:T(8,128)}, f32[768,384]{1,0:T(8,128)S(1)}, u32[]{:S(2)}, u32[]{:S(2)}) collective-permute-start(f32[768,384]{1,0:T(8,128)} %get-tuple-element.857.refs_2_), channel_id=1, source_target_pairs={{0,16},{8,24},{16,0},{24,8},{1,17},{9,25},{17,1},{25,9},{2,18},{10... | collective-permute-start | bytes 3538952 | tf_op jit(solution)/shard_map/ppermute | solution.py:319
  19.7 51.1 %collective-permute-start.31 = (f32[768,384]{1,0:T(8,128)}, f32[768,384]{1,0:T(8,128)}, u32[]{:S(2)}, u32[]{:S(2)}) collective-permute-start(f32[768,384]{1,0:T(8,128)} %get-tuple-element.859.refs_3_), channel_id=1, source_target_pairs={{0,24},{8,16},{16,8},{24,0},{1,25},{9,17},{17,9},{25,1},{2,26},{10... | collective-permute-start | bytes 3538952 | tf_op jit(solution)/shard_map/ppermute | solution.py:319
  30.2 41.3 %collective-permute-start.32 = (f32[768,384]{1,0:T(8,128)}, f32[768,384]{1,0:T(8,128)}, u32[]{:S(2)}, u32[]{:S(2)}) collective-permute-start(f32[768,384]{1,0:T(8,128)} %get-tuple-element.1173.refs_0_), channel_id=1, source_target_pairs={{0,1},{1,0},{2,3},{3,2},{4,5},{5,4},{6,7},{7,6},{8,9},{9,8},{10,11... | collective-permute-start | bytes 3538952 | tf_op jit(solution)/shard_map/ppermute | solution.py:322
  110.5 70.3 %collective-permute-start.39 = (f32[38,128,128]{2,1,0:T(8,128)}, f32[38,128,128]{2,1,0:T(8,128)S(1)}, u32[]{:S(2)}, u32[]{:S(2)}) collective-permute-start(f32[38,128,128]{2,1,0:T(8,128)} %get-tuple-element.457), channel_id=1, source_target_pairs={{0,8},{1,17},{2,10},{3,19},{4,12},{5,21},{6,14},{7,23},{8,0},{9,25... | collective-permute-start | bytes 7471112 | tf_op jit(solution)/shard_map/ppermute | solution.py:403
  114.4 66.4 %collective-permute-start.40 = (f32[38,128,128]{2,1,0:T(8,128)}, f32[38,128,128]{2,1,0:T(8,128)S(1)}, u32[]{:S(2)}, u32[]{:S(2)}) collective-permute-start(f32[38,128,128]{2,1,0:T(8,128)} %get-tuple-element.457), channel_id=1, source_target_pairs={{0,16},{1,9},{2,18},{3,11},{4,20},{5,13},{6,22},{7,15},{8,24},{9,1... | collective-permute-start | bytes 7471112 | tf_op jit(solution)/shard_map/ppermute | solution.py:403
  114.5 62.2 %collective-permute-start.41 = (f32[12,128,128]{2,1,0:T(8,128)}, f32[12,128,128]{2,1,0:T(8,128)S(1)}, u32[]{:S(2)}, u32[]{:S(2)}) collective-permute-start(f32[12,128,128]{2,1,0:T(8,128)} %get-tuple-element.459.refs_1_), channel_id=1, source_target_pairs={{0,16},{1,9},{2,18},{3,11},{4,20},{5,13},{6,22},{7,15},{8,24},{9,1... | collective-permute-start | bytes 2359304 | tf_op jit(solution)/shard_map/ppermute | solution.py:403
  116.4 70.0 %collective-permute-start.36 = (f32[38,128,128]{2,1,0:T(8,128)}, f32[38,128,128]{2,1,0:T(8,128)}, u32[]{:S(2)}, u32[]{:S(2)}) collective-permute-start(f32[38,128,128]{2,1,0:T(8,128)} %copy-done.39), channel_id=1, source_target_pairs={{0,2},{1,3},{2,6},{3,7},{6,4},{7,5},{4,0},{5,1},{8,10},{9,11},{10,... | collective-permute-start | bytes 7471112 | tf_op jit(solution)/shard_map/ppermute | solution.py:325
  183.7 30.6 %collective-permute-start.42 = (f32[38,128,128]{2,1,0:T(8,128)}, f32[38,128,128]{2,1,0:T(8,128)}, u32[]{:S(2)}, u32[]{:S(2)}) collective-permute-start(f32[38,128,128]{2,1,0:T(8,128)} %get-tuple-element.461.refs_0_), channel_id=1, source_target_pairs={{0,16},{1,9},{2,18},{3,11},{4,20},{5,13},{6,22},{7,15},{8,24},{9,1... | collective-permute-start | bytes 7471112 | tf_op jit(solution)/shard_map/ppermute | solution.py:403
  185.1 82.6 %collective-permute-start.46 = (f32[20,128,128]{2,1,0:T(8,128)S(1)}, f32[20,128,128]{2,1,0:T(8,128)S(1)}, u32[]{:S(2)}, u32[]{:S(2)}) collective-permute-start(f32[20,128,128]{2,1,0:T(8,128)S(1)} %copy-done.20), channel_id=1, source_target_pairs={{0,2},{1,3},{2,6},{3,7},{6,4},{7,5},{4,0},{5,1},{8,10},{9,11},{10,... | collective-permute-start | bytes 3932168 | tf_op jit(solution)/shard_map/ppermute | solution.py:325
  214.3 56.6 %collective-permute-start.44 = (f32[38,128,128]{2,1,0:T(8,128)}, f32[38,128,128]{2,1,0:T(8,128)}, u32[]{:S(2)}, u32[]{:S(2)}) collective-permute-start(f32[38,128,128]{2,1,0:T(8,128)} %get-tuple-element.462.refs_0_), channel_id=1, source_target_pairs={{0,8},{1,17},{2,10},{3,19},{4,12},{5,21},{6,14},{7,23},{8,0},{9,25... | collective-permute-start | bytes 7471112 | tf_op jit(solution)/shard_map/ppermute | solution.py:403
  214.5 56.4 %collective-permute-start.45 = (f32[38,128,128]{2,1,0:T(8,128)}, f32[38,128,128]{2,1,0:T(8,128)}, u32[]{:S(2)}, u32[]{:S(2)}) collective-permute-start(f32[38,128,128]{2,1,0:T(8,128)} %get-tuple-element.462.refs_0_), channel_id=1, source_target_pairs={{0,16},{1,9},{2,18},{3,11},{4,20},{5,13},{6,22},{7,15},{8,24},{9,1... | collective-permute-start | bytes 7471112 | tf_op jit(solution)/shard_map/ppermute | solution.py:403
  215.8 72.2 %collective-permute-start.43 = (f32[38,128,128]{2,1,0:T(8,128)}, f32[38,128,128]{2,1,0:T(8,128)}, u32[]{:S(2)}, u32[]{:S(2)}) collective-permute-start(f32[38,128,128]{2,1,0:T(8,128)} %get-tuple-element.462.refs_0_), channel_id=1, source_target_pairs={{0,2},{1,3},{2,6},{3,7},{6,4},{7,5},{4,0},{5,1},{8,10},{9,11},{10,... | collective-permute-start | bytes 7471112 | tf_op jit(solution)/shard_map/ppermute | solution.py:325
  270.9 30.5 %collective-permute-start.47 = (f32[38,128,128]{2,1,0:T(8,128)}, f32[38,128,128]{2,1,0:T(8,128)S(1)}, u32[]{:S(2)}, u32[]{:S(2)}) collective-permute-start(f32[38,128,128]{2,1,0:T(8,128)} %get-tuple-element.469.refs_0_), channel_id=1, source_target_pairs={{0,16},{1,9},{2,18},{3,11},{4,20},{5,13},{6,22},{7,15},{8,24},{9,1... | collective-permute-start | bytes 7471112 | tf_op jit(solution)/shard_map/ppermute | solution.py:403
  271.6 78.5 %collective-permute-start.51 = (f32[20,128,128]{2,1,0:T(8,128)}, f32[20,128,128]{2,1,0:T(8,128)}, u32[]{:S(2)}, u32[]{:S(2)}) collective-permute-start(f32[20,128,128]{2,1,0:T(8,128)} %copy-done.34), channel_id=1, source_target_pairs={{0,2},{1,3},{2,6},{3,7},{6,4},{7,5},{4,0},{5,1},{8,10},{9,11},{10,... | collective-permute-start | bytes 3932168 | tf_op jit(solution)/shard_map/ppermute | solution.py:325
  302.7 55.6 %collective-permute-start.49 = (f32[38,128,128]{2,1,0:T(8,128)}, f32[38,128,128]{2,1,0:T(8,128)S(1)}, u32[]{:S(2)}, u32[]{:S(2)}) collective-permute-start(f32[38,128,128]{2,1,0:T(8,128)} %get-tuple-element.470.refs_0_), channel_id=1, source_target_pairs={{0,8},{1,17},{2,10},{3,19},{4,12},{5,21},{6,14},{7,23},{8,0},{9,25... | collective-permute-start | bytes 7471112 | tf_op jit(solution)/shard_map/ppermute | solution.py:403
  303.2 55.2 %collective-permute-start.50 = (f32[38,128,128]{2,1,0:T(8,128)}, f32[38,128,128]{2,1,0:T(8,128)}, u32[]{:S(2)}, u32[]{:S(2)}) collective-permute-start(f32[38,128,128]{2,1,0:T(8,128)} %get-tuple-element.470.refs_0_), channel_id=1, source_target_pairs={{0,16},{1,9},{2,18},{3,11},{4,20},{5,13},{6,22},{7,15},{8,24},{9,1... | collective-permute-start | bytes 7471112 | tf_op jit(solution)/shard_map/ppermute | solution.py:403
  304.3 72.5 %collective-permute-start.48 = (f32[38,128,128]{2,1,0:T(8,128)}, f32[38,128,128]{2,1,0:T(8,128)}, u32[]{:S(2)}, u32[]{:S(2)}) collective-permute-start(f32[38,128,128]{2,1,0:T(8,128)} %get-tuple-element.470.refs_0_), channel_id=1, source_target_pairs={{0,2},{1,3},{2,6},{3,7},{6,4},{7,5},{4,0},{5,1},{8,10},{9,11},{10,... | collective-permute-start | bytes 7471112 | tf_op jit(solution)/shard_map/ppermute | solution.py:325
  359.8 30.5 %collective-permute-start.52 = (f32[38,128,128]{2,1,0:T(8,128)}, f32[38,128,128]{2,1,0:T(8,128)S(1)}, u32[]{:S(2)}, u32[]{:S(2)}) collective-permute-start(f32[38,128,128]{2,1,0:T(8,128)} %get-tuple-element.479.refs_0_), channel_id=1, source_target_pairs={{0,16},{1,9},{2,18},{3,11},{4,20},{5,13},{6,22},{7,15},{8,24},{9,1... | collective-permute-start | bytes 7471112 | tf_op jit(solution)/shard_map/ppermute | solution.py:403
  361.1 79.6 %collective-permute-start.55 = (f32[20,128,128]{2,1,0:T(8,128)}, f32[20,128,128]{2,1,0:T(8,128)}, u32[]{:S(2)}, u32[]{:S(2)}) collective-permute-start(f32[20,128,128]{2,1,0:T(8,128)} %collective-permute-done.51.refs_3_.refs_1_.refs_2_), channel_id=1, source_target_pairs={{0,2},{1,3},{2,6},{3,7},{6,4},{7,5},{4,0},{5,1},{8,10},{9,11},{10,... | collective-permute-start | bytes 3932168 | tf_op jit(solution)/shard_map/ppermute | solution.py:325
  391.7 53.9 %collective-permute-start.53 = (f32[38,128,128]{2,1,0:T(8,128)}, f32[38,128,128]{2,1,0:T(8,128)}, u32[]{:S(2)}, u32[]{:S(2)}) collective-permute-start(f32[38,128,128]{2,1,0:T(8,128)} %get-tuple-element.480.refs_0_), channel_id=1, source_target_pairs={{0,8},{1,17},{2,10},{3,19},{4,12},{5,21},{6,14},{7,23},{8,0},{9,25... | collective-permute-start | bytes 7471112 | tf_op jit(solution)/shard_map/ppermute | solution.py:403
  392.4 53.2 %collective-permute-start.54 = (f32[38,128,128]{2,1,0:T(8,128)}, f32[38,128,128]{2,1,0:T(8,128)}, u32[]{:S(2)}, u32[]{:S(2)}) collective-permute-start(f32[38,128,128]{2,1,0:T(8,128)} %get-tuple-element.480.refs_0_), channel_id=1, source_target_pairs={{0,16},{1,9},{2,18},{3,11},{4,20},{5,13},{6,22},{7,15},{8,24},{9,1... | collective-permute-start | bytes 7471112 | tf_op jit(solution)/shard_map/ppermute | solution.py:403
  460.5 30.5 %collective-permute-start.57 = (f32[38,128,128]{2,1,0:T(8,128)}, f32[38,128,128]{2,1,0:T(8,128)S(1)}, u32[]{:S(2)}, u32[]{:S(2)}) collective-permute-start(f32[38,128,128]{2,1,0:T(8,128)} %get-tuple-element.490.refs_0_), channel_id=1, source_target_pairs={{0,16},{1,9},{2,18},{3,11},{4,20},{5,13},{6,22},{7,15},{8,24},{9,1... | collective-permute-start | bytes 7471112 | tf_op jit(solution)/shard_map/ppermute | solution.py:403
  (64 other events, 738.5 us)

commit v2 on v1

--- a/solution.py
+++ b/solution.py
@@ -377,9 +377,9 @@
     )
     ends = jnp.sum(own[:, :, None, :] * (ids[None, :] < (jnp.arange(per_chip + 1) * CORES * kd)[:, None]), axis=-1)
 
-    straight = max(2, round(tiles * 38 / 72)) if R == 4 else max(4, 2 * round(tiles * 25 / 72))
-    extra = max(2, round(tiles * 12 / 72)) if R == 4 else 0
-    pooled = max(R, round(tiles * 20 / 72)) if R == 4 else 0
+    straight = max(2, round(tiles * 37 / 72)) if R == 4 else max(4, 2 * round(tiles * 25 / 72))
+    extra = max(2, round(tiles * 13 / 72)) if R == 4 else 0
+    pooled = max(R, round(tiles * 23 / 72)) if R == 4 else 0
     longest = tiles + straight + extra
     slots = jnp.pad(slots, ((0, 0), (0, 0), (0, longest - tiles)), constant_values=-1)
     most = jnp.max(cores_counts)
@@ -498,26 +498,28 @@
             pools.append(by_plane(pools[0]))
             received = []
             for step in range(Z):
-                first_near, mine = gate([first_near, mine], [second_near, pools[step]])
-                third_near = across(first_near, 2)
                 mixed = (pools[step], straight, end, True, None)
-                near = [(first_near, 0, straight, False, 0), (second_near, 0, straight, False, 1), mixed]
-                last = [(third_near, 0, straight, False, None), mixed]
                 if step:
                     home = [(along[step], 0, straight, False, None), mixed]
                     mine, others[0] = add(mine, others[0], step, [0], home)
                 if step == Z - 1:
                     received.append(by_core(others[0]))
+                first_near, mine = gate([first_near, mine], [second_near, pools[step], along[step if step else 1]])
+                third_near = across(first_near, 2)
+                near = [(first_near, 0, straight, False, 0), (second_near, 0, straight, False, 1), mixed]
+                last = [(third_near, 0, straight, False, None), mixed]
+                mine, others[1] = add(mine, others[1], step, [1, 2], near)
+                if step == Z - 1:
+                    received.append(by_core(others[1]))
+                    mine = place(received_at[0], wide, mine, received[0])
                 else:
-                    along[step + 1], mine = gate([along[step + 1], mine], [third_near])
+                    along[step + 1], pools[step + 1], mine = gate(
+                        [along[step + 1], pools[step + 1], mine], [third_near]
+                    )
                     first_near, second_near = across(along[step + 1], 1), across(along[step + 1], 2)
                     if step + 2 < Z:
                         along.append(by_plane(along[step + 1]))
                         pools.append(by_plane(pools[step + 1]))
-                mine, others[1] = add(mine, others[1], step, [1, 2], near)
-                if step == Z - 1:
-                    received.append(by_core(others[1]))
-                    mine = place(received_at[0], wide, mine, received[0])
                 mine, others[2] = add(mine, others[2], step, [3], last)
             received.append(by_core(others[2]))
             mine = place(received_at[1:3].reshape(-1), wide, mine, received[1])

time: 531 us -> 521 us (0.981)
  Pallas kernels: 287 us -> 281 us
    ppermute x15, waiting for transfers between devices: 132 us -> 105 us  [across(): lax.ppermute(x, ('row', 'col'), [(a * devices + d, (a ^ (near if d % CORE...]
    ppermute x6, waiting for transfers between devices: 0.02 us -> 22 us  [by_plane(): lax.ppermute(x, 'col', [(ring[a] * CORES + c, ring[(a + 1) % Z] * CORES +...]
    pallas_call x12, Pallas kernels: 241 us -> 233 us  [multiply(): pl.pallas_call(functools.partial(multiply_kernel, at=at, turn=turn, first...]
    unnamed x107 -> x95, local copies, waits for them, and re-layouts: 19.3 us -> 18.3 us
  transfers between devices with their start and end apart: 36 -> 36, of which waited for: 13 -> 14; matrix products, arithmetic and copies ran while one was open for 5% -> 5% of each run, Pallas kernels for 50% -> 52%
where the time goes in v2:
time: 521 us; the launch traced here: 511 us
  Pallas kernels  281 us (54%)
  waiting for transfers between devices  150 us (29%)
  starting transfers between devices  34.3 us (7%)
  local copies, waits for them, and re-layouts  32.9 us (6%)
  other arithmetic  8.6 us (2%)
    pallas_call x12, Pallas kernels, multiply(): pl.pallas_call(functools.partial(multiply_kernel, at=at, turn=turn, first...  233 us
    ppermute x15, waiting for transfers between devices, across(): lax.ppermute(x, ('row', 'col'), [(a * devices + d, (a ^ (near if d % CORE...  105 us
    pallas_call x1, Pallas kernels, split_amplitudes(): pl.pallas_call(functools.partial(split_kernel, second=second, deep=deep),...  24.3 us
    ppermute x6, waiting for transfers between devices, by_plane(): lax.ppermute(x, 'col', [(ring[a] * CORES + c, ring[(a + 1) % Z] * CORES +...  22 us
    unnamed x95, local copies, waits for them, and re-layouts  18.3 us
    ppermute x6, waiting for transfers between devices, by_row(): return lax.ppermute(x, 'row', [(a, a ^ distance) for a in range(R)])  16.2 us
    ppermute x15, starting transfers between devices, across(): lax.ppermute(x, ('row', 'col'), [(a * devices + d, (a ^ (near if d % CORE...  13.1 us
    ppermute x6, starting transfers between devices, by_plane(): lax.ppermute(x, 'col', [(ring[a] * CORES + c, ring[(a + 1) % Z] * CORES +...  12 us
  transfers between devices with their start and end apart: 36, of which 14 were waited for; matrix products, arithmetic and copies ran while one was open for 5% of the time, Pallas kernels for 52%

profile of v2, /device:TPU:0, one launch (start us, length us, event | category | flops | bytes accessed | tf_op | source)
XLA Modules:
  0.0 511.1 jit_solution(7052374144168044667)
XLA Ops:
  1.8 4.6 fusion.28
  29.6 24.3 %shard_map.101 = (bf16[48,1024,256]{2,1,0:T(8,128)(2,1)}, f32[512,6144]{1,0:T(8,128)}) custom-call(s32[16,48]{1,0:T(8,128)S(1)} %copy-done.34, s32[16,48]{1,0:T(8,128)S(1)} %collective-permute-done.27.other_pattern, f32[512,6144]{1,0:T(8,128)} %bitcast.176, f32[512,6144]{1,0:T(8,128)} %collective-permute-done.28.other_ref, s32[1106]{0:T(1024)S(1)} %concatenate.19.lists_ref), custom_call_target="tpu_custom_call" | custom-call | flops 25165824 | bytes 62914560 | tf_op jit(solution)/shard_map/pallas_call | solution.py:44
  53.9 16.2 %collective-permute-done.30.refs_1_ = f32[768,384]{1,0:T(8,128)S(1)} collective-permute-done((f32[768,384]{1,0:T(8,128)}, f32[768,384]{1,0:T(8,128)S(1)}, u32[]{:S(2)}, u32[]{:S(2)}) %collective-permute-start.30) | collective-permute-done | bytes 1179680 | tf_op jit(solution)/shard_map/ppermute | solution.py:319
  76.7 10.8 %shard_map.103 = (f32[37,128,128]{2,1,0:T(8,128)}, f32[13,128,128]{2,1,0:T(8,128)S(1)}, f32[37,128,128]{2,1,0:T(8,128)S(1)}) custom-call(s32[1106]{0:T(1024)S(1)} %concatenate.19.lists_ref, f32[768,384]{1,0:T(8,128)} %get-tuple-element.1194.refs_0_, f32[768,384]{1,0:T(8,128)S(1)} %get-tuple-element.1195.refs_1_, f32[768,384]{1,0:T(8,128)S(1)} %get-tuple-element.1196.refs_2_, ...), custom_call_target="tpu_custom_call" | custom-call | bytes 15138816 | tf_op jit(solution)/shard_map/pallas_call | solution.py:80
  93.8 14.1 %shard_map.104 = (f32[512,6144]{1,0:T(8,128)}, f32[512,768]{1,0:T(8,128)}) custom-call(s32[1106]{0:T(1024)S(1)} %concatenate.19.lists_ref, bf16[48,1024,256]{2,1,0:T(8,128)(2,1)} %get-tuple-element.1202.refs_3_.amp_ref, f32[512,6144]{1,0:T(8,128)} %get-tuple-element.461.mine_in, ...), custom_call_target="tpu_custom_call", output_to_operand_aliasing={{0}: (2, {}), {1}: (3, {})} | custom-call | flops 16106127360 | bytes 3932160 | tf_op jit(solution)/shard_map/pallas_call | solution.py:235
  116.4 59.3 %collective-permute-done.39.refs_3_ = f32[13,128,128]{2,1,0:T(8,128)S(1)} collective-permute-done((f32[13,128,128]{2,1,0:T(8,128)}, f32[13,128,128]{2,1,0:T(8,128)S(1)}, u32[]{:S(2)}, u32[]{:S(2)}) %collective-permute-start.39) | collective-permute-done | bytes 852000 | tf_op jit(solution)/shard_map/ppermute | solution.py:403
  186.5 24.1 %shard_map.108 = (f32[512,6144]{1,0:T(8,128)}, f32[512,1536]{1,0:T(8,128)}) custom-call(s32[1106]{0:T(1024)S(1)} %concatenate.19.lists_ref, bf16[48,1024,256]{2,1,0:T(8,128)(2,1)} %get-tuple-element.1202.refs_3_.amp_ref, f32[512,6144]{1,0:T(8,128)} %get-tuple-element.466.mine_in, ...), custom_call_target="tpu_custom_call", output_to_operand_aliasing={{0}: (2, {}), {1}: (3, {})} | custom-call | flops 32212254720 | bytes 7864320 | tf_op jit(solution)/shard_map/pallas_call | solution.py:235
  210.6 6.6 %collective-permute-done.40.refs_1_ = f32[23,128,128]{2,1,0:T(8,128)} collective-permute-done((f32[23,128,128]{2,1,0:T(8,128)}, f32[23,128,128]{2,1,0:T(8,128)}, u32[]{:S(2)}, u32[]{:S(2)}) %collective-permute-start.40) | collective-permute-done | bytes 1507360 | tf_op jit(solution)/shard_map/ppermute | solution.py:325
  228.2 17.6 %shard_map.110 = (f32[512,6144]{1,0:T(8,128)}, f32[512,768]{1,0:T(8,128)}) custom-call(s32[1106]{0:T(1024)S(1)} %concatenate.19.lists_ref, bf16[48,1024,256]{2,1,0:T(8,128)(2,1)} %get-tuple-element.1202.refs_3_.amp_ref, f32[512,6144]{1,0:T(8,128)} %get-tuple-element.471.mine_in, ...), custom_call_target="tpu_custom_call", output_to_operand_aliasing={{0}: (2, {}), {1}: (3, {})} | custom-call | flops 16106127360 | bytes 3932160 | tf_op jit(solution)/shard_map/pallas_call | solution.py:235
  245.9 17.5 %shard_map.111 = (f32[512,6144]{1,0:T(8,128)}, f32[512,768]{1,0:T(8,128)}) custom-call(s32[1106]{0:T(1024)S(1)} %concatenate.19.lists_ref, bf16[48,1024,256]{2,1,0:T(8,128)(2,1)} %get-tuple-element.1202.refs_3_.amp_ref, f32[512,6144]{1,0:T(8,128)} %get-tuple-element.472.mine_in, ...), custom_call_target="tpu_custom_call", output_to_operand_aliasing={{0}: (2, {}), {1}: (3, {})} | custom-call | flops 16106127360 | bytes 3932160 | tf_op jit(solution)/shard_map/pallas_call | solution.py:235
  263.4 11.0 %collective-permute-done.46.refs_0_ = f32[37,128,128]{2,1,0:T(8,128)} collective-permute-done((f32[37,128,128]{2,1,0:T(8,128)}, f32[37,128,128]{2,1,0:T(8,128)}, u32[]{:S(2)}, u32[]{:S(2)}) %collective-permute-start.46) | collective-permute-done | bytes 2424864 | tf_op jit(solution)/shard_map/ppermute | solution.py:403
  274.8 24.8 %shard_map.113 = (f32[512,6144]{1,0:T(8,128)}, f32[512,1536]{1,0:T(8,128)}) custom-call(s32[1106]{0:T(1024)S(1)} %concatenate.19.lists_ref, bf16[48,1024,256]{2,1,0:T(8,128)(2,1)} %get-tuple-element.1202.refs_3_.amp_ref, f32[512,6144]{1,0:T(8,128)} %get-tuple-element.475.mine_in, ...), custom_call_target="tpu_custom_call", output_to_operand_aliasing={{0}: (2, {}), {1}: (3, {})} | custom-call | flops 32212254720 | bytes 7864320 | tf_op jit(solution)/shard_map/pallas_call | solution.py:235
  299.6 8.5 %collective-permute-done.45.refs_1_ = f32[23,128,128]{2,1,0:T(8,128)} collective-permute-done((f32[23,128,128]{2,1,0:T(8,128)}, f32[23,128,128]{2,1,0:T(8,128)}, u32[]{:S(2)}, u32[]{:S(2)}) %collective-permute-start.45) | collective-permute-done | bytes 1507360 | tf_op jit(solution)/shard_map/ppermute | solution.py:325
  317.3 18.5 %shard_map.115 = (f32[512,6144]{1,0:T(8,128)}, f32[512,768]{1,0:T(8,128)}) custom-call(s32[1106]{0:T(1024)S(1)} %concatenate.19.lists_ref, bf16[48,1024,256]{2,1,0:T(8,128)(2,1)} %get-tuple-element.1202.refs_3_.amp_ref, f32[512,6144]{1,0:T(8,128)} %get-tuple-element.481.mine_in, ...), custom_call_target="tpu_custom_call", output_to_operand_aliasing={{0}: (2, {}), {1}: (3, {})} | custom-call | flops 16106127360 | bytes 3932160 | tf_op jit(solution)/shard_map/pallas_call | solution.py:235
  335.8 15.4 %shard_map.116 = (f32[512,6144]{1,0:T(8,128)}, f32[512,768]{1,0:T(8,128)}) custom-call(s32[1106]{0:T(1024)S(1)} %concatenate.19.lists_ref, bf16[48,1024,256]{2,1,0:T(8,128)(2,1)} %get-tuple-element.1202.refs_3_.amp_ref, f32[512,6144]{1,0:T(8,128)} %get-tuple-element.483.mine_in, ...), custom_call_target="tpu_custom_call", output_to_operand_aliasing={{0}: (2, {}), {1}: (3, {})} | custom-call | flops 16106127360 | bytes 3932160 | tf_op jit(solution)/shard_map/pallas_call | solution.py:235
  351.2 12.6 %collective-permute-done.51.refs_0_ = f32[37,128,128]{2,1,0:T(8,128)} collective-permute-done((f32[37,128,128]{2,1,0:T(8,128)}, f32[37,128,128]{2,1,0:T(8,128)}, u32[]{:S(2)}, u32[]{:S(2)}) %collective-permute-start.51) | collective-permute-done | bytes 2424864 | tf_op jit(solution)/shard_map/ppermute | solution.py:403
  364.3 25.9 %shard_map.118 = (f32[512,6144]{1,0:T(8,128)}, f32[512,1536]{1,0:T(8,128)}) custom-call(s32[1106]{0:T(1024)S(1)} %concatenate.19.lists_ref, bf16[48,1024,256]{2,1,0:T(8,128)(2,1)} %get-tuple-element.1202.refs_3_.amp_ref, f32[512,6144]{1,0:T(8,128)} %get-tuple-element.486.mine_in, ...), custom_call_target="tpu_custom_call", output_to_operand_aliasing={{0}: (2, {}), {1}: (3, {})} | custom-call | flops 32212254720 | bytes 7864320 | tf_op jit(solution)/shard_map/pallas_call | solution.py:235
  390.3 6.9 %collective-permute-done.50.refs_1_ = f32[23,128,128]{2,1,0:T(8,128)} collective-permute-done((f32[23,128,128]{2,1,0:T(8,128)}, f32[23,128,128]{2,1,0:T(8,128)}, u32[]{:S(2)}, u32[]{:S(2)}) %collective-permute-start.50) | collective-permute-done | bytes 1507360 | tf_op jit(solution)/shard_map/ppermute | solution.py:325
  400.7 15.5 %shard_map.120 = (f32[512,6144]{1,0:T(8,128)}, f32[512,768]{1,0:T(8,128)}) custom-call(s32[1106]{0:T(1024)S(1)} %concatenate.19.lists_ref, bf16[48,1024,256]{2,1,0:T(8,128)(2,1)} %get-tuple-element.1202.refs_3_.amp_ref, f32[512,6144]{1,0:T(8,128)} %get-tuple-element.491.mine_in, ...), custom_call_target="tpu_custom_call", output_to_operand_aliasing={{0}: (2, {}), {1}: (3, {})} | custom-call | flops 16106127360 | bytes 3932160 | tf_op jit(solution)/shard_map/pallas_call | solution.py:235
  416.2 17.3 %shard_map.121 = (f32[512,6144]{1,0:T(8,128)}, f32[512,768]{1,0:T(8,128)}) custom-call(s32[1106]{0:T(1024)S(1)} %concatenate.19.lists_ref, bf16[48,1024,256]{2,1,0:T(8,128)(2,1)} %get-tuple-element.1202.refs_3_.amp_ref, f32[512,6144]{1,0:T(8,128)} %get-tuple-element.493.mine_in, ...), custom_call_target="tpu_custom_call", output_to_operand_aliasing={{0}: (2, {}), {1}: (3, {})} | custom-call | flops 16106127360 | bytes 3932160 | tf_op jit(solution)/shard_map/pallas_call | solution.py:235
  433.6 18.5 %collective-permute-done.54.refs_0_ = f32[37,128,128]{2,1,0:T(8,128)} collective-permute-done((f32[37,128,128]{2,1,0:T(8,128)}, f32[37,128,128]{2,1,0:T(8,128)}, u32[]{:S(2)}, u32[]{:S(2)}) %collective-permute-start.54) | collective-permute-done | bytes 2424864 | tf_op jit(solution)/shard_map/ppermute | solution.py:403
  452.7 24.0 %shard_map.123 = (f32[512,6144]{1,0:T(8,128)}, f32[512,1536]{1,0:T(8,128)}) custom-call(s32[1106]{0:T(1024)S(1)} %concatenate.19.lists_ref, bf16[48,1024,256]{2,1,0:T(8,128)(2,1)} %get-tuple-element.1202.refs_3_.amp_ref, f32[512,6144]{1,0:T(8,128)} %get-tuple-element.497.mine_in, ...), custom_call_target="tpu_custom_call", output_to_operand_aliasing={{0}: (2, {}), {1}: (3, {})} | custom-call | flops 32212254720 | bytes 7864320 | tf_op jit(solution)/shard_map/pallas_call | solution.py:235
  481.9 17.7 %shard_map.125 = (f32[512,6144]{1,0:T(8,128)}, f32[512,768]{1,0:T(8,128)}) custom-call(s32[1106]{0:T(1024)S(1)} %concatenate.19.lists_ref, bf16[48,1024,256]{2,1,0:T(8,128)(2,1)} %get-tuple-element.1202.refs_3_.amp_ref, f32[512,6144]{1,0:T(8,128)} %shard_map.124.mine_in, ...), custom_call_target="tpu_custom_call", output_to_operand_aliasing={{0}: (2, {}), {1}: (3, {})} | custom-call | flops 16106127360 | bytes 3932160 | tf_op jit(solution)/shard_map/pallas_call | solution.py:235
  500.1 4.8 shard_map.126.mine_in
  (257 shorter events, 91.7 us)
Async XLA Ops:
  15.2 38.7 %collective-permute-start.29 = (f32[768,384]{1,0:T(8,128)}, f32[768,384]{1,0:T(8,128)S(1)}, u32[]{:S(2)}, u32[]{:S(2)}) collective-permute-start(f32[768,384]{1,0:T(8,128)} %get-tuple-element.873.refs_1_), channel_id=1, source_target_pairs={{0,8},{8,0},{16,24},{24,16},{1,9},{9,1},{17,25},{25,17},{2,10},{10... | collective-permute-start | bytes 3538952 | tf_op jit(solution)/shard_map/ppermute | solution.py:319
  17.4 52.8 %collective-permute-start.30 = (f32[768,384]{1,0:T(8,128)}, f32[768,384]{1,0:T(8,128)S(1)}, u32[]{:S(2)}, u32[]{:S(2)}) collective-permute-start(f32[768,384]{1,0:T(8,128)} %get-tuple-element.872.refs_2_), channel_id=1, source_target_pairs={{0,16},{8,24},{16,0},{24,8},{1,17},{9,25},{17,1},{25,9},{2,18},{10... | collective-permute-start | bytes 3538952 | tf_op jit(solution)/shard_map/ppermute | solution.py:319
  19.1 51.1 %collective-permute-start.31 = (f32[768,384]{1,0:T(8,128)}, f32[768,384]{1,0:T(8,128)}, u32[]{:S(2)}, u32[]{:S(2)}) collective-permute-start(f32[768,384]{1,0:T(8,128)} %get-tuple-element.874.refs_3_), channel_id=1, source_target_pairs={{0,24},{8,16},{16,8},{24,0},{1,25},{9,17},{17,9},{25,1},{2,26},{10... | collective-permute-start | bytes 3538952 | tf_op jit(solution)/shard_map/ppermute | solution.py:319
  29.4 41.4 %collective-permute-start.32 = (f32[768,384]{1,0:T(8,128)}, f32[768,384]{1,0:T(8,128)}, u32[]{:S(2)}, u32[]{:S(2)}) collective-permute-start(f32[768,384]{1,0:T(8,128)} %get-tuple-element.1194.refs_0_), channel_id=1, source_target_pairs={{0,1},{1,0},{2,3},{3,2},{4,5},{5,4},{6,7},{7,6},{8,9},{9,8},{10,11... | collective-permute-start | bytes 3538952 | tf_op jit(solution)/shard_map/ppermute | solution.py:322
  91.0 91.6 %collective-permute-start.36 = (f32[37,128,128]{2,1,0:T(8,128)}, f32[37,128,128]{2,1,0:T(8,128)S(1)}, u32[]{:S(2)}, u32[]{:S(2)}) collective-permute-start(f32[37,128,128]{2,1,0:T(8,128)} %get-tuple-element.458.refs_0_), channel_id=1, source_target_pairs={{0,2},{1,3},{2,6},{3,7},{6,4},{7,5},{4,0},{5,1},{8,10},{9,11},{10,... | collective-permute-start | bytes 7274504 | tf_op jit(solution)/shard_map/ppermute | solution.py:325
  112.3 70.3 %collective-permute-start.41 = (f32[37,128,128]{2,1,0:T(8,128)}, f32[37,128,128]{2,1,0:T(8,128)}, u32[]{:S(2)}, u32[]{:S(2)}) collective-permute-start(f32[37,128,128]{2,1,0:T(8,128)} %get-tuple-element.464), channel_id=1, source_target_pairs={{0,8},{1,17},{2,10},{3,19},{4,12},{5,21},{6,14},{7,23},{8,0},{9,25... | collective-permute-start | bytes 7274504 | tf_op jit(solution)/shard_map/ppermute | solution.py:403
  113.5 69.1 %collective-permute-start.42 = (f32[37,128,128]{2,1,0:T(8,128)}, f32[37,128,128]{2,1,0:T(8,128)}, u32[]{:S(2)}, u32[]{:S(2)}) collective-permute-start(f32[37,128,128]{2,1,0:T(8,128)} %get-tuple-element.464), channel_id=1, source_target_pairs={{0,16},{1,9},{2,18},{3,11},{4,20},{5,13},{6,22},{7,15},{8,24},{9,1... | collective-permute-start | bytes 7274504 | tf_op jit(solution)/shard_map/ppermute | solution.py:403
  114.6 61.1 %collective-permute-start.39 = (f32[13,128,128]{2,1,0:T(8,128)}, f32[13,128,128]{2,1,0:T(8,128)S(1)}, u32[]{:S(2)}, u32[]{:S(2)}) collective-permute-start(f32[13,128,128]{2,1,0:T(8,128)} %get-tuple-element.463.refs_1_), channel_id=1, source_target_pairs={{0,16},{1,9},{2,18},{3,11},{4,20},{5,13},{6,22},{7,15},{8,24},{9,1... | collective-permute-start | bytes 2555912 | tf_op jit(solution)/shard_map/ppermute | solution.py:403
  181.0 36.2 %collective-permute-start.40 = (f32[23,128,128]{2,1,0:T(8,128)}, f32[23,128,128]{2,1,0:T(8,128)}, u32[]{:S(2)}, u32[]{:S(2)}) collective-permute-start(f32[23,128,128]{2,1,0:T(8,128)} %shard_map.106.refs_3_.refs_2_.refs_1_), channel_id=1, source_target_pairs={{0,2},{1,3},{2,6},{3,7},{6,4},{7,5},{4,0},{5,1},{8,10},{9,11},{10,... | collective-permute-start | bytes 4521992 | tf_op jit(solution)/shard_map/ppermute | solution.py:325
  184.0 33.2 %collective-permute-start.43 = (f32[37,128,128]{2,1,0:T(8,128)}, f32[37,128,128]{2,1,0:T(8,128)S(1)}, u32[]{:S(2)}, u32[]{:S(2)}) collective-permute-start(f32[37,128,128]{2,1,0:T(8,128)} %get-tuple-element.467.refs_0_), channel_id=1, source_target_pairs={{0,16},{1,9},{2,18},{3,11},{4,20},{5,13},{6,22},{7,15},{8,24},{9,1... | collective-permute-start | bytes 7274504 | tf_op jit(solution)/shard_map/ppermute | solution.py:403
  218.7 55.6 %collective-permute-start.46 = (f32[37,128,128]{2,1,0:T(8,128)}, f32[37,128,128]{2,1,0:T(8,128)}, u32[]{:S(2)}, u32[]{:S(2)}) collective-permute-start(f32[37,128,128]{2,1,0:T(8,128)} %get-tuple-element.469.refs_0_.refs_4_), channel_id=1, source_target_pairs={{0,8},{1,17},{2,10},{3,19},{4,12},{5,21},{6,14},{7,23},{8,0},{9,25... | collective-permute-start | bytes 7274504 | tf_op jit(solution)/shard_map/ppermute | solution.py:403
  220.0 54.4 %collective-permute-start.47 = (f32[37,128,128]{2,1,0:T(8,128)}, f32[37,128,128]{2,1,0:T(8,128)}, u32[]{:S(2)}, u32[]{:S(2)}) collective-permute-start(f32[37,128,128]{2,1,0:T(8,128)} %get-tuple-element.469.refs_0_.refs_4_), channel_id=1, source_target_pairs={{0,16},{1,9},{2,18},{3,11},{4,20},{5,13},{6,22},{7,15},{8,24},{9,1... | collective-permute-start | bytes 7274504 | tf_op jit(solution)/shard_map/ppermute | solution.py:403
  220.9 87.2 %collective-permute-start.44 = (f32[37,128,128]{2,1,0:T(8,128)}, f32[37,128,128]{2,1,0:T(8,128)}, u32[]{:S(2)}, u32[]{:S(2)}) collective-permute-start(f32[37,128,128]{2,1,0:T(8,128)} %get-tuple-element.469.refs_0_.refs_4_), channel_id=1, source_target_pairs={{0,2},{1,3},{2,6},{3,7},{6,4},{7,5},{4,0},{5,1},{8,10},{9,11},{10,... | collective-permute-start | bytes 7274504 | tf_op jit(solution)/shard_map/ppermute | solution.py:325
  221.9 86.1 %collective-permute-start.45 = (f32[23,128,128]{2,1,0:T(8,128)}, f32[23,128,128]{2,1,0:T(8,128)}, u32[]{:S(2)}, u32[]{:S(2)}) collective-permute-start(f32[23,128,128]{2,1,0:T(8,128)} %get-tuple-element.470.refs_1_.refs_3_.refs_2_), channel_id=1, source_target_pairs={{0,2},{1,3},{2,6},{3,7},{6,4},{7,5},{4,0},{5,1},{8,10},{9,11},{10,... | collective-permute-start | bytes 4521992 | tf_op jit(solution)/shard_map/ppermute | solution.py:325
  274.4 33.7 %collective-permute-start.48 = (f32[37,128,128]{2,1,0:T(8,128)}, f32[37,128,128]{2,1,0:T(8,128)S(1)}, u32[]{:S(2)}, u32[]{:S(2)}) collective-permute-start(f32[37,128,128]{2,1,0:T(8,128)} %get-tuple-element.477.refs_0_), channel_id=1, source_target_pairs={{0,16},{1,9},{2,18},{3,11},{4,20},{5,13},{6,22},{7,15},{8,24},{9,1... | collective-permute-start | bytes 7274504 | tf_op jit(solution)/shard_map/ppermute | solution.py:403
  309.5 54.3 %collective-permute-start.51 = (f32[37,128,128]{2,1,0:T(8,128)}, f32[37,128,128]{2,1,0:T(8,128)}, u32[]{:S(2)}, u32[]{:S(2)}) collective-permute-start(f32[37,128,128]{2,1,0:T(8,128)} %get-tuple-element.479.refs_0_.refs_4_), channel_id=1, source_target_pairs={{0,8},{1,17},{2,10},{3,19},{4,12},{5,21},{6,14},{7,23},{8,0},{9,25... | collective-permute-start | bytes 7274504 | tf_op jit(solution)/shard_map/ppermute | solution.py:403
  310.7 53.1 %collective-permute-start.52 = (f32[37,128,128]{2,1,0:T(8,128)}, f32[37,128,128]{2,1,0:T(8,128)}, u32[]{:S(2)}, u32[]{:S(2)}) collective-permute-start(f32[37,128,128]{2,1,0:T(8,128)} %get-tuple-element.479.refs_0_.refs_4_), channel_id=1, source_target_pairs={{0,16},{1,9},{2,18},{3,11},{4,20},{5,13},{6,22},{7,15},{8,24},{9,1... | collective-permute-start | bytes 7274504 | tf_op jit(solution)/shard_map/ppermute | solution.py:403
  311.1 86.1 %collective-permute-start.49 = (f32[37,128,128]{2,1,0:T(8,128)}, f32[37,128,128]{2,1,0:T(8,128)S(1)}, u32[]{:S(2)}, u32[]{:S(2)}) collective-permute-start(f32[37,128,128]{2,1,0:T(8,128)} %get-tuple-element.479.refs_0_.refs_4_), channel_id=1, source_target_pairs={{0,2},{1,3},{2,6},{3,7},{6,4},{7,5},{4,0},{5,1},{8,10},{9,11},{10,... | collective-permute-start | bytes 7274504 | tf_op jit(solution)/shard_map/ppermute | solution.py:325
  312.0 85.2 %collective-permute-start.50 = (f32[23,128,128]{2,1,0:T(8,128)}, f32[23,128,128]{2,1,0:T(8,128)}, u32[]{:S(2)}, u32[]{:S(2)}) collective-permute-start(f32[23,128,128]{2,1,0:T(8,128)} %get-tuple-element.480.refs_1_.refs_3_.refs_2_), channel_id=1, source_target_pairs={{0,2},{1,3},{2,6},{3,7},{6,4},{7,5},{4,0},{5,1},{8,10},{9,11},{10,... | collective-permute-start | bytes 4521992 | tf_op jit(solution)/shard_map/ppermute | solution.py:325
  363.8 33.4 %collective-permute-start.53 = (f32[37,128,128]{2,1,0:T(8,128)}, f32[37,128,128]{2,1,0:T(8,128)}, u32[]{:S(2)}, u32[]{:S(2)}) collective-permute-start(f32[37,128,128]{2,1,0:T(8,128)} %get-tuple-element.488.refs_0_), channel_id=1, source_target_pairs={{0,16},{1,9},{2,18},{3,11},{4,20},{5,13},{6,22},{7,15},{8,24},{9,1... | collective-permute-start | bytes 7274504 | tf_op jit(solution)/shard_map/ppermute | solution.py:403
  398.6 53.5 %collective-permute-start.54 = (f32[37,128,128]{2,1,0:T(8,128)}, f32[37,128,128]{2,1,0:T(8,128)}, u32[]{:S(2)}, u32[]{:S(2)}) collective-permute-start(f32[37,128,128]{2,1,0:T(8,128)} %get-tuple-element.490.refs_0_.refs_4_), channel_id=1, source_target_pairs={{0,8},{1,17},{2,10},{3,19},{4,12},{5,21},{6,14},{7,23},{8,0},{9,25... | collective-permute-start | bytes 7274504 | tf_op jit(solution)/shard_map/ppermute | solution.py:403
  400.2 51.9 %collective-permute-start.55 = (f32[37,128,128]{2,1,0:T(8,128)}, f32[37,128,128]{2,1,0:T(8,128)}, u32[]{:S(2)}, u32[]{:S(2)}) collective-permute-start(f32[37,128,128]{2,1,0:T(8,128)} %get-tuple-element.490.refs_0_.refs_4_), channel_id=1, source_target_pairs={{0,16},{1,9},{2,18},{3,11},{4,20},{5,13},{6,22},{7,15},{8,24},{9,1... | collective-permute-start | bytes 7274504 | tf_op jit(solution)/shard_map/ppermute | solution.py:403
  433.6 43.3 %collective-permute-start.56 = (f32[512,768]{1,0:T(8,128)}, f32[512,768]{1,0:T(8,128)}, u32[]{:S(2)}, u32[]{:S(2)}) collective-permute-start(f32[512,768]{1,0:T(8,128)} %get-tuple-element.501), channel_id=1, source_target_pairs={{0,1},{1,0},{2,3},{3,2},{4,5},{5,4},{6,7},{7,6},{8,9},{9,8},{10,11... | collective-permute-start | bytes 4718600 | tf_op jit(solution)/shard_map/ppermute | solution.py:322
  452.1 29.8 %collective-permute-start.57 = (f32[37,128,128]{2,1,0:T(8,128)}, f32[37,128,128]{2,1,0:T(8,128)S(1)}, u32[]{:S(2)}, u32[]{:S(2)}) collective-permute-start(f32[37,128,128]{2,1,0:T(8,128)} %get-tuple-element.499.refs_0_), channel_id=1, source_target_pairs={{0,16},{1,9},{2,18},{3,11},{4,20},{5,13},{6,22},{7,15},{8,24},{9,1... | collective-permute-start | bytes 7274504 | tf_op jit(solution)/shard_map/ppermute | solution.py:403
  (58 other events, 566.0 us)

commit v3 on v2

--- a/solution.py
+++ b/solution.py
@@ -377,9 +377,9 @@
     )
     ends = jnp.sum(own[:, :, None, :] * (ids[None, :] < (jnp.arange(per_chip + 1) * CORES * kd)[:, None]), axis=-1)
 
-    straight = max(2, round(tiles * 37 / 72)) if R == 4 else max(4, 2 * round(tiles * 25 / 72))
-    extra = max(2, round(tiles * 13 / 72)) if R == 4 else 0
-    pooled = max(R, round(tiles * 23 / 72)) if R == 4 else 0
+    straight = max(2, round(tiles * 38 / 72)) if R == 4 else max(4, 2 * round(tiles * 25 / 72))
+    extra = max(2, round(tiles * 12 / 72)) if R == 4 else 0
+    pooled = max(R, round(tiles * 20 / 72)) if R == 4 else 0
     longest = tiles + straight + extra
     slots = jnp.pad(slots, ((0, 0), (0, 0), (0, longest - tiles)), constant_values=-1)
     most = jnp.max(cores_counts)

time: 521 us -> 517 us (level)
  waiting for transfers between devices: 150 us -> 138 us
  Pallas kernels: 281 us -> 290 us
    ppermute x6, waiting for transfers between devices: 22 us -> 5.14 us  [by_plane(): lax.ppermute(x, 'col', [(ring[a] * CORES + c, ring[(a + 1) % Z] * CORES +...]
    pallas_call x12, Pallas kernels: 233 us -> 241 us  [multiply(): pl.pallas_call(functools.partial(multiply_kernel, at=at, turn=turn, first...]
    ppermute x6, starting transfers between devices: 12 us -> 4.09 us  [by_plane(): lax.ppermute(x, 'col', [(ring[a] * CORES + c, ring[(a + 1) % Z] * CORES +...]
    ppermute x15, starting transfers between devices: 13.1 us -> 19.3 us  [across(): lax.ppermute(x, ('row', 'col'), [(a * devices + d, (a ^ (near if d % CORE...]
  transfers between devices with their start and end apart: 36 -> 36, of which waited for: 14 -> 17; matrix products, arithmetic and copies ran while one was open for 5% -> 5% of each run, Pallas kernels for 52% -> 54%
where the time goes in v3:
time: 517 us; the launch traced here: 509 us
  Pallas kernels  290 us (56%)
  waiting for transfers between devices  138 us (27%)
  starting transfers between devices  35.3 us (7%)
  local copies, waits for them, and re-layouts  32.5 us (6%)
  other arithmetic  8.62 us (2%)
    pallas_call x12, Pallas kernels, multiply(): pl.pallas_call(functools.partial(multiply_kernel, at=at, turn=turn, first...  241 us
    ppermute x15, waiting for transfers between devices, across(): lax.ppermute(x, ('row', 'col'), [(a * devices + d, (a ^ (near if d % CORE...  111 us
    pallas_call x1, Pallas kernels, split_amplitudes(): pl.pallas_call(functools.partial(split_kernel, second=second, deep=deep),...  24.3 us
    ppermute x15, starting transfers between devices, across(): lax.ppermute(x, ('row', 'col'), [(a * devices + d, (a ^ (near if d % CORE...  19.3 us
    unnamed x95, local copies, waits for them, and re-layouts  17.9 us
    ppermute x6, waiting for transfers between devices, by_row(): return lax.ppermute(x, 'row', [(a, a ^ distance) for a in range(R)])  16.2 us
    pallas_call x3, Pallas kernels, place(): pl.pallas_call(place_kernel, grid_spec=pltpu.PrefetchScalarGridSpec(num_s...  11.7 us
    pallas_call x1, Pallas kernels, pack(): pl.pallas_call(functools.partial(pack_kernel, plan=plan, sources=len(sour...  10.9 us
  transfers between devices with their start and end apart: 36, of which 17 were waited for; matrix products, arithmetic and copies ran while one was open for 5% of the time, Pallas kernels for 54%

profile of v3, /device:TPU:0, one launch (start us, length us, event | category | flops | bytes accessed | tf_op | source)
XLA Modules:
  0.0 508.9 jit_solution(17691766851176320247)
XLA Ops:
  1.8 4.6 fusion.28
  21.3 3.7 fusion.20
  29.6 24.3 %shard_map.101 = (bf16[48,1024,256]{2,1,0:T(8,128)(2,1)}, f32[512,6144]{1,0:T(8,128)}) custom-call(s32[16,48]{1,0:T(8,128)S(1)} %copy-done.34, s32[16,48]{1,0:T(8,128)S(1)} %collective-permute-done.27.other_pattern, f32[512,6144]{1,0:T(8,128)} %bitcast.176, f32[512,6144]{1,0:T(8,128)} %collective-permute-done.28.other_ref, s32[1106]{0:T(1024)S(1)} %concatenate.19.lists_ref), custom_call_target="tpu_custom_call" | custom-call | flops 25165824 | bytes 62914560 | tf_op jit(solution)/shard_map/pallas_call | solution.py:44
  54.0 16.2 %collective-permute-done.30.refs_1_ = f32[768,384]{1,0:T(8,128)S(1)} collective-permute-done((f32[768,384]{1,0:T(8,128)}, f32[768,384]{1,0:T(8,128)S(1)}, u32[]{:S(2)}, u32[]{:S(2)}) %collective-permute-start.30) | collective-permute-done | bytes 1179680 | tf_op jit(solution)/shard_map/ppermute | solution.py:319
  76.7 10.9 %shard_map.103 = (f32[38,128,128]{2,1,0:T(8,128)}, f32[12,128,128]{2,1,0:T(8,128)S(1)}, f32[38,128,128]{2,1,0:T(8,128)S(1)}) custom-call(s32[1106]{0:T(1024)S(1)} %concatenate.19.lists_ref, f32[768,384]{1,0:T(8,128)} %get-tuple-element.1194.refs_0_, f32[768,384]{1,0:T(8,128)S(1)} %get-tuple-element.1195.refs_1_, f32[768,384]{1,0:T(8,128)S(1)} %get-tuple-element.1196.refs_2_, ...), custom_call_target="tpu_custom_call" | custom-call | bytes 15204352 | tf_op jit(solution)/shard_map/pallas_call | solution.py:80
  94.0 14.8 %shard_map.104 = (f32[512,6144]{1,0:T(8,128)}, f32[512,768]{1,0:T(8,128)}) custom-call(s32[1106]{0:T(1024)S(1)} %concatenate.19.lists_ref, bf16[48,1024,256]{2,1,0:T(8,128)(2,1)} %get-tuple-element.1202.refs_3_.amp_ref, f32[512,6144]{1,0:T(8,128)} %get-tuple-element.461.mine_in, ...), custom_call_target="tpu_custom_call", output_to_operand_aliasing={{0}: (2, {}), {1}: (3, {})} | custom-call | flops 16106127360 | bytes 3932160 | tf_op jit(solution)/shard_map/pallas_call | solution.py:235
  115.6 60.8 %collective-permute-done.39.refs_3_ = f32[12,128,128]{2,1,0:T(8,128)S(1)} collective-permute-done((f32[12,128,128]{2,1,0:T(8,128)}, f32[12,128,128]{2,1,0:T(8,128)S(1)}, u32[]{:S(2)}, u32[]{:S(2)}) %collective-permute-start.39) | collective-permute-done | bytes 786464 | tf_op jit(solution)/shard_map/ppermute | solution.py:403
  186.5 26.6 %shard_map.108 = (f32[512,6144]{1,0:T(8,128)}, f32[512,1536]{1,0:T(8,128)}) custom-call(s32[1106]{0:T(1024)S(1)} %concatenate.19.lists_ref, bf16[48,1024,256]{2,1,0:T(8,128)(2,1)} %get-tuple-element.1202.refs_3_.amp_ref, f32[512,6144]{1,0:T(8,128)} %get-tuple-element.466.mine_in, ...), custom_call_target="tpu_custom_call", output_to_operand_aliasing={{0}: (2, {}), {1}: (3, {})} | custom-call | flops 32212254720 | bytes 7864320 | tf_op jit(solution)/shard_map/pallas_call | solution.py:235
  223.5 17.4 %shard_map.110 = (f32[512,6144]{1,0:T(8,128)}, f32[512,768]{1,0:T(8,128)}) custom-call(s32[1106]{0:T(1024)S(1)} %concatenate.19.lists_ref, bf16[48,1024,256]{2,1,0:T(8,128)(2,1)} %get-tuple-element.1202.refs_3_.amp_ref, f32[512,6144]{1,0:T(8,128)} %get-tuple-element.471.mine_in, ...), custom_call_target="tpu_custom_call", output_to_operand_aliasing={{0}: (2, {}), {1}: (3, {})} | custom-call | flops 16106127360 | bytes 3932160 | tf_op jit(solution)/shard_map/pallas_call | solution.py:235
  240.9 18.8 %shard_map.111 = (f32[512,6144]{1,0:T(8,128)}, f32[512,768]{1,0:T(8,128)}) custom-call(s32[1106]{0:T(1024)S(1)} %concatenate.19.lists_ref, bf16[48,1024,256]{2,1,0:T(8,128)(2,1)} %get-tuple-element.1202.refs_3_.amp_ref, f32[512,6144]{1,0:T(8,128)} %get-tuple-element.472.mine_in, ...), custom_call_target="tpu_custom_call", output_to_operand_aliasing={{0}: (2, {}), {1}: (3, {})} | custom-call | flops 16106127360 | bytes 3932160 | tf_op jit(solution)/shard_map/pallas_call | solution.py:235
  259.7 13.6 %collective-permute-done.46.refs_0_ = f32[38,128,128]{2,1,0:T(8,128)} collective-permute-done((f32[38,128,128]{2,1,0:T(8,128)}, f32[38,128,128]{2,1,0:T(8,128)}, u32[]{:S(2)}, u32[]{:S(2)}) %collective-permute-start.46) | collective-permute-done | bytes 2490400 | tf_op jit(solution)/shard_map/ppermute | solution.py:403
  274.8 26.5 %shard_map.113 = (f32[512,6144]{1,0:T(8,128)}, f32[512,1536]{1,0:T(8,128)}) custom-call(s32[1106]{0:T(1024)S(1)} %concatenate.19.lists_ref, bf16[48,1024,256]{2,1,0:T(8,128)(2,1)} %get-tuple-element.1202.refs_3_.amp_ref, f32[512,6144]{1,0:T(8,128)} %get-tuple-element.475.mine_in, ...), custom_call_target="tpu_custom_call", output_to_operand_aliasing={{0}: (2, {}), {1}: (3, {})} | custom-call | flops 32212254720 | bytes 7864320 | tf_op jit(solution)/shard_map/pallas_call | solution.py:235
  311.0 20.0 %shard_map.115 = (f32[512,6144]{1,0:T(8,128)}, f32[512,768]{1,0:T(8,128)}) custom-call(s32[1106]{0:T(1024)S(1)} %concatenate.19.lists_ref, bf16[48,1024,256]{2,1,0:T(8,128)(2,1)} %get-tuple-element.1202.refs_3_.amp_ref, f32[512,6144]{1,0:T(8,128)} %get-tuple-element.481.mine_in, ...), custom_call_target="tpu_custom_call", output_to_operand_aliasing={{0}: (2, {}), {1}: (3, {})} | custom-call | flops 16106127360 | bytes 3932160 | tf_op jit(solution)/shard_map/pallas_call | solution.py:235
  331.0 15.4 %shard_map.116 = (f32[512,6144]{1,0:T(8,128)}, f32[512,768]{1,0:T(8,128)}) custom-call(s32[1106]{0:T(1024)S(1)} %concatenate.19.lists_ref, bf16[48,1024,256]{2,1,0:T(8,128)(2,1)} %get-tuple-element.1202.refs_3_.amp_ref, f32[512,6144]{1,0:T(8,128)} %get-tuple-element.483.mine_in, ...), custom_call_target="tpu_custom_call", output_to_operand_aliasing={{0}: (2, {}), {1}: (3, {})} | custom-call | flops 16106127360 | bytes 3932160 | tf_op jit(solution)/shard_map/pallas_call | solution.py:235
  346.4 15.6 %collective-permute-done.51.refs_0_ = f32[38,128,128]{2,1,0:T(8,128)} collective-permute-done((f32[38,128,128]{2,1,0:T(8,128)}, f32[38,128,128]{2,1,0:T(8,128)}, u32[]{:S(2)}, u32[]{:S(2)}) %collective-permute-start.51) | collective-permute-done | bytes 2490400 | tf_op jit(solution)/shard_map/ppermute | solution.py:403
  362.9 26.6 %shard_map.118 = (f32[512,6144]{1,0:T(8,128)}, f32[512,1536]{1,0:T(8,128)}) custom-call(s32[1106]{0:T(1024)S(1)} %concatenate.19.lists_ref, bf16[48,1024,256]{2,1,0:T(8,128)(2,1)} %get-tuple-element.1202.refs_3_.amp_ref, f32[512,6144]{1,0:T(8,128)} %get-tuple-element.486.mine_in, ...), custom_call_target="tpu_custom_call", output_to_operand_aliasing={{0}: (2, {}), {1}: (3, {})} | custom-call | flops 32212254720 | bytes 7864320 | tf_op jit(solution)/shard_map/pallas_call | solution.py:235
  395.1 16.2 %shard_map.120 = (f32[512,6144]{1,0:T(8,128)}, f32[512,768]{1,0:T(8,128)}) custom-call(s32[1106]{0:T(1024)S(1)} %concatenate.19.lists_ref, bf16[48,1024,256]{2,1,0:T(8,128)(2,1)} %get-tuple-element.1202.refs_3_.amp_ref, f32[512,6144]{1,0:T(8,128)} %get-tuple-element.491.mine_in, ...), custom_call_target="tpu_custom_call", output_to_operand_aliasing={{0}: (2, {}), {1}: (3, {})} | custom-call | flops 16106127360 | bytes 3932160 | tf_op jit(solution)/shard_map/pallas_call | solution.py:235
  411.3 18.0 %shard_map.121 = (f32[512,6144]{1,0:T(8,128)}, f32[512,768]{1,0:T(8,128)}) custom-call(s32[1106]{0:T(1024)S(1)} %concatenate.19.lists_ref, bf16[48,1024,256]{2,1,0:T(8,128)(2,1)} %get-tuple-element.1202.refs_3_.amp_ref, f32[512,6144]{1,0:T(8,128)} %get-tuple-element.493.mine_in, ...), custom_call_target="tpu_custom_call", output_to_operand_aliasing={{0}: (2, {}), {1}: (3, {})} | custom-call | flops 16106127360 | bytes 3932160 | tf_op jit(solution)/shard_map/pallas_call | solution.py:235
  429.4 18.3 %collective-permute-done.54.refs_0_ = f32[38,128,128]{2,1,0:T(8,128)} collective-permute-done((f32[38,128,128]{2,1,0:T(8,128)}, f32[38,128,128]{2,1,0:T(8,128)}, u32[]{:S(2)}, u32[]{:S(2)}) %collective-permute-start.54) | collective-permute-done | bytes 2490400 | tf_op jit(solution)/shard_map/ppermute | solution.py:403
  449.5 24.6 %shard_map.123 = (f32[512,6144]{1,0:T(8,128)}, f32[512,1536]{1,0:T(8,128)}) custom-call(s32[1106]{0:T(1024)S(1)} %concatenate.19.lists_ref, bf16[48,1024,256]{2,1,0:T(8,128)(2,1)} %get-tuple-element.1202.refs_3_.amp_ref, f32[512,6144]{1,0:T(8,128)} %get-tuple-element.497.mine_in, ...), custom_call_target="tpu_custom_call", output_to_operand_aliasing={{0}: (2, {}), {1}: (3, {})} | custom-call | flops 32212254720 | bytes 7864320 | tf_op jit(solution)/shard_map/pallas_call | solution.py:235
  474.2 3.4 shard_map.124.mine_in
  478.2 16.5 %shard_map.125 = (f32[512,6144]{1,0:T(8,128)}, f32[512,768]{1,0:T(8,128)}) custom-call(s32[1106]{0:T(1024)S(1)} %concatenate.19.lists_ref, bf16[48,1024,256]{2,1,0:T(8,128)(2,1)} %get-tuple-element.1202.refs_3_.amp_ref, f32[512,6144]{1,0:T(8,128)} %shard_map.124.mine_in, ...), custom_call_target="tpu_custom_call", output_to_operand_aliasing={{0}: (2, {}), {1}: (3, {})} | custom-call | flops 16106127360 | bytes 3932160 | tf_op jit(solution)/shard_map/pallas_call | solution.py:235
  497.8 4.8 shard_map.126.mine_in
  502.7 3.5 shard_map.127
  (257 shorter events, 85.2 us)
Async XLA Ops:
  15.3 38.7 %collective-permute-start.29 = (f32[768,384]{1,0:T(8,128)}, f32[768,384]{1,0:T(8,128)S(1)}, u32[]{:S(2)}, u32[]{:S(2)}) collective-permute-start(f32[768,384]{1,0:T(8,128)} %get-tuple-element.873.refs_1_), channel_id=1, source_target_pairs={{0,8},{8,0},{16,24},{24,16},{1,9},{9,1},{17,25},{25,17},{2,10},{10... | collective-permute-start | bytes 3538952 | tf_op jit(solution)/shard_map/ppermute | solution.py:319
  17.4 52.8 %collective-permute-start.30 = (f32[768,384]{1,0:T(8,128)}, f32[768,384]{1,0:T(8,128)S(1)}, u32[]{:S(2)}, u32[]{:S(2)}) collective-permute-start(f32[768,384]{1,0:T(8,128)} %get-tuple-element.872.refs_2_), channel_id=1, source_target_pairs={{0,16},{8,24},{16,0},{24,8},{1,17},{9,25},{17,1},{25,9},{2,18},{10... | collective-permute-start | bytes 3538952 | tf_op jit(solution)/shard_map/ppermute | solution.py:319
  19.1 51.1 %collective-permute-start.31 = (f32[768,384]{1,0:T(8,128)}, f32[768,384]{1,0:T(8,128)}, u32[]{:S(2)}, u32[]{:S(2)}) collective-permute-start(f32[768,384]{1,0:T(8,128)} %get-tuple-element.874.refs_3_), channel_id=1, source_target_pairs={{0,24},{8,16},{16,8},{24,0},{1,25},{9,17},{17,9},{25,1},{2,26},{10... | collective-permute-start | bytes 3538952 | tf_op jit(solution)/shard_map/ppermute | solution.py:319
  29.5 41.4 %collective-permute-start.32 = (f32[768,384]{1,0:T(8,128)}, f32[768,384]{1,0:T(8,128)}, u32[]{:S(2)}, u32[]{:S(2)}) collective-permute-start(f32[768,384]{1,0:T(8,128)} %get-tuple-element.1194.refs_0_), channel_id=1, source_target_pairs={{0,1},{1,0},{2,3},{3,2},{4,5},{5,4},{6,7},{7,6},{8,9},{9,8},{10,11... | collective-permute-start | bytes 3538952 | tf_op jit(solution)/shard_map/ppermute | solution.py:322
  91.2 91.1 %collective-permute-start.36 = (f32[38,128,128]{2,1,0:T(8,128)}, f32[38,128,128]{2,1,0:T(8,128)S(1)}, u32[]{:S(2)}, u32[]{:S(2)}) collective-permute-start(f32[38,128,128]{2,1,0:T(8,128)} %get-tuple-element.458.refs_0_), channel_id=1, source_target_pairs={{0,2},{1,3},{2,6},{3,7},{6,4},{7,5},{4,0},{5,1},{8,10},{9,11},{10,... | collective-permute-start | bytes 7471112 | tf_op jit(solution)/shard_map/ppermute | solution.py:325
  111.0 71.3 %collective-permute-start.41 = (f32[38,128,128]{2,1,0:T(8,128)}, f32[38,128,128]{2,1,0:T(8,128)}, u32[]{:S(2)}, u32[]{:S(2)}) collective-permute-start(f32[38,128,128]{2,1,0:T(8,128)} %get-tuple-element.464), channel_id=1, source_target_pairs={{0,8},{1,17},{2,10},{3,19},{4,12},{5,21},{6,14},{7,23},{8,0},{9,25... | collective-permute-start | bytes 7471112 | tf_op jit(solution)/shard_map/ppermute | solution.py:403
  112.7 69.6 %collective-permute-start.42 = (f32[38,128,128]{2,1,0:T(8,128)}, f32[38,128,128]{2,1,0:T(8,128)}, u32[]{:S(2)}, u32[]{:S(2)}) collective-permute-start(f32[38,128,128]{2,1,0:T(8,128)} %get-tuple-element.464), channel_id=1, source_target_pairs={{0,16},{1,9},{2,18},{3,11},{4,20},{5,13},{6,22},{7,15},{8,24},{9,1... | collective-permute-start | bytes 7471112 | tf_op jit(solution)/shard_map/ppermute | solution.py:403
  114.2 62.2 %collective-permute-start.39 = (f32[12,128,128]{2,1,0:T(8,128)}, f32[12,128,128]{2,1,0:T(8,128)S(1)}, u32[]{:S(2)}, u32[]{:S(2)}) collective-permute-start(f32[12,128,128]{2,1,0:T(8,128)} %get-tuple-element.463.refs_1_), channel_id=1, source_target_pairs={{0,16},{1,9},{2,18},{3,11},{4,20},{5,13},{6,22},{7,15},{8,24},{9,1... | collective-permute-start | bytes 2359304 | tf_op jit(solution)/shard_map/ppermute | solution.py:403
  181.5 32.0 %collective-permute-start.40 = (f32[20,128,128]{2,1,0:T(8,128)}, f32[20,128,128]{2,1,0:T(8,128)}, u32[]{:S(2)}, u32[]{:S(2)}) collective-permute-start(f32[20,128,128]{2,1,0:T(8,128)} %shard_map.106.refs_3_.refs_2_.refs_1_), channel_id=1, source_target_pairs={{0,2},{1,3},{2,6},{3,7},{6,4},{7,5},{4,0},{5,1},{8,10},{9,11},{10,... | collective-permute-start | bytes 3932168 | tf_op jit(solution)/shard_map/ppermute | solution.py:325
  183.8 30.5 %collective-permute-start.43 = (f32[38,128,128]{2,1,0:T(8,128)}, f32[38,128,128]{2,1,0:T(8,128)S(1)}, u32[]{:S(2)}, u32[]{:S(2)}) collective-permute-start(f32[38,128,128]{2,1,0:T(8,128)} %get-tuple-element.467.refs_0_), channel_id=1, source_target_pairs={{0,16},{1,9},{2,18},{3,11},{4,20},{5,13},{6,22},{7,15},{8,24},{9,1... | collective-permute-start | bytes 7471112 | tf_op jit(solution)/shard_map/ppermute | solution.py:403
  215.7 57.6 %collective-permute-start.46 = (f32[38,128,128]{2,1,0:T(8,128)}, f32[38,128,128]{2,1,0:T(8,128)}, u32[]{:S(2)}, u32[]{:S(2)}) collective-permute-start(f32[38,128,128]{2,1,0:T(8,128)} %get-tuple-element.469.refs_0_.refs_4_), channel_id=1, source_target_pairs={{0,8},{1,17},{2,10},{3,19},{4,12},{5,21},{6,14},{7,23},{8,0},{9,25... | collective-permute-start | bytes 7471112 | tf_op jit(solution)/shard_map/ppermute | solution.py:403
  218.4 54.9 %collective-permute-start.47 = (f32[38,128,128]{2,1,0:T(8,128)}, f32[38,128,128]{2,1,0:T(8,128)}, u32[]{:S(2)}, u32[]{:S(2)}) collective-permute-start(f32[38,128,128]{2,1,0:T(8,128)} %get-tuple-element.469.refs_0_.refs_4_), channel_id=1, source_target_pairs={{0,16},{1,9},{2,18},{3,11},{4,20},{5,13},{6,22},{7,15},{8,24},{9,1... | collective-permute-start | bytes 7471112 | tf_op jit(solution)/shard_map/ppermute | solution.py:403
  219.6 83.9 %collective-permute-start.44 = (f32[38,128,128]{2,1,0:T(8,128)}, f32[38,128,128]{2,1,0:T(8,128)}, u32[]{:S(2)}, u32[]{:S(2)}) collective-permute-start(f32[38,128,128]{2,1,0:T(8,128)} %get-tuple-element.469.refs_0_.refs_4_), channel_id=1, source_target_pairs={{0,2},{1,3},{2,6},{3,7},{6,4},{7,5},{4,0},{5,1},{8,10},{9,11},{10,... | collective-permute-start | bytes 7471112 | tf_op jit(solution)/shard_map/ppermute | solution.py:325
  219.9 83.6 %collective-permute-start.45 = (f32[20,128,128]{2,1,0:T(8,128)}, f32[20,128,128]{2,1,0:T(8,128)}, u32[]{:S(2)}, u32[]{:S(2)}) collective-permute-start(f32[20,128,128]{2,1,0:T(8,128)} %get-tuple-element.470.refs_1_.refs_3_.refs_2_), channel_id=1, source_target_pairs={{0,2},{1,3},{2,6},{3,7},{6,4},{7,5},{4,0},{5,1},{8,10},{9,11},{10,... | collective-permute-start | bytes 3932168 | tf_op jit(solution)/shard_map/ppermute | solution.py:325
  273.3 30.5 %collective-permute-start.48 = (f32[38,128,128]{2,1,0:T(8,128)}, f32[38,128,128]{2,1,0:T(8,128)S(1)}, u32[]{:S(2)}, u32[]{:S(2)}) collective-permute-start(f32[38,128,128]{2,1,0:T(8,128)} %get-tuple-element.477.refs_0_), channel_id=1, source_target_pairs={{0,16},{1,9},{2,18},{3,11},{4,20},{5,13},{6,22},{7,15},{8,24},{9,1... | collective-permute-start | bytes 7471112 | tf_op jit(solution)/shard_map/ppermute | solution.py:403
  305.2 56.8 %collective-permute-start.51 = (f32[38,128,128]{2,1,0:T(8,128)}, f32[38,128,128]{2,1,0:T(8,128)}, u32[]{:S(2)}, u32[]{:S(2)}) collective-permute-start(f32[38,128,128]{2,1,0:T(8,128)} %get-tuple-element.479.refs_0_.refs_4_), channel_id=1, source_target_pairs={{0,8},{1,17},{2,10},{3,19},{4,12},{5,21},{6,14},{7,23},{8,0},{9,25... | collective-permute-start | bytes 7471112 | tf_op jit(solution)/shard_map/ppermute | solution.py:403
  306.6 55.3 %collective-permute-start.52 = (f32[38,128,128]{2,1,0:T(8,128)}, f32[38,128,128]{2,1,0:T(8,128)}, u32[]{:S(2)}, u32[]{:S(2)}) collective-permute-start(f32[38,128,128]{2,1,0:T(8,128)} %get-tuple-element.479.refs_0_.refs_4_), channel_id=1, source_target_pairs={{0,16},{1,9},{2,18},{3,11},{4,20},{5,13},{6,22},{7,15},{8,24},{9,1... | collective-permute-start | bytes 7471112 | tf_op jit(solution)/shard_map/ppermute | solution.py:403
  308.4 83.7 %collective-permute-start.49 = (f32[38,128,128]{2,1,0:T(8,128)}, f32[38,128,128]{2,1,0:T(8,128)S(1)}, u32[]{:S(2)}, u32[]{:S(2)}) collective-permute-start(f32[38,128,128]{2,1,0:T(8,128)} %get-tuple-element.479.refs_0_.refs_4_), channel_id=1, source_target_pairs={{0,2},{1,3},{2,6},{3,7},{6,4},{7,5},{4,0},{5,1},{8,10},{9,11},{10,... | collective-permute-start | bytes 7471112 | tf_op jit(solution)/shard_map/ppermute | solution.py:325
  308.4 83.7 %collective-permute-start.50 = (f32[20,128,128]{2,1,0:T(8,128)}, f32[20,128,128]{2,1,0:T(8,128)}, u32[]{:S(2)}, u32[]{:S(2)}) collective-permute-start(f32[20,128,128]{2,1,0:T(8,128)} %get-tuple-element.480.refs_1_.refs_3_.refs_2_), channel_id=1, source_target_pairs={{0,2},{1,3},{2,6},{3,7},{6,4},{7,5},{4,0},{5,1},{8,10},{9,11},{10,... | collective-permute-start | bytes 3932168 | tf_op jit(solution)/shard_map/ppermute | solution.py:325
  362.0 30.6 %collective-permute-start.53 = (f32[38,128,128]{2,1,0:T(8,128)}, f32[38,128,128]{2,1,0:T(8,128)}, u32[]{:S(2)}, u32[]{:S(2)}) collective-permute-start(f32[38,128,128]{2,1,0:T(8,128)} %get-tuple-element.488.refs_0_), channel_id=1, source_target_pairs={{0,16},{1,9},{2,18},{3,11},{4,20},{5,13},{6,22},{7,15},{8,24},{9,1... | collective-permute-start | bytes 7471112 | tf_op jit(solution)/shard_map/ppermute | solution.py:403
  393.5 54.2 %collective-permute-start.54 = (f32[38,128,128]{2,1,0:T(8,128)}, f32[38,128,128]{2,1,0:T(8,128)}, u32[]{:S(2)}, u32[]{:S(2)}) collective-permute-start(f32[38,128,128]{2,1,0:T(8,128)} %get-tuple-element.490.refs_0_.refs_4_), channel_id=1, source_target_pairs={{0,8},{1,17},{2,10},{3,19},{4,12},{5,21},{6,14},{7,23},{8,0},{9,25... | collective-permute-start | bytes 7471112 | tf_op jit(solution)/shard_map/ppermute | solution.py:403
  394.2 53.6 %collective-permute-start.55 = (f32[38,128,128]{2,1,0:T(8,128)}, f32[38,128,128]{2,1,0:T(8,128)}, u32[]{:S(2)}, u32[]{:S(2)}) collective-permute-start(f32[38,128,128]{2,1,0:T(8,128)} %get-tuple-element.490.refs_0_.refs_4_), channel_id=1, source_target_pairs={{0,16},{1,9},{2,18},{3,11},{4,20},{5,13},{6,22},{7,15},{8,24},{9,1... | collective-permute-start | bytes 7471112 | tf_op jit(solution)/shard_map/ppermute | solution.py:403
  429.3 44.8 %collective-permute-start.56 = (f32[512,768]{1,0:T(8,128)}, f32[512,768]{1,0:T(8,128)}, u32[]{:S(2)}, u32[]{:S(2)}) collective-permute-start(f32[512,768]{1,0:T(8,128)} %get-tuple-element.501), channel_id=1, source_target_pairs={{0,1},{1,0},{2,3},{3,2},{4,5},{5,4},{6,7},{7,6},{8,9},{9,8},{10,11... | collective-permute-start | bytes 4718600 | tf_op jit(solution)/shard_map/ppermute | solution.py:322
  447.7 30.5 %collective-permute-start.57 = (f32[38,128,128]{2,1,0:T(8,128)}, f32[38,128,128]{2,1,0:T(8,128)S(1)}, u32[]{:S(2)}, u32[]{:S(2)}) collective-permute-start(f32[38,128,128]{2,1,0:T(8,128)} %get-tuple-element.499.refs_0_), channel_id=1, source_target_pairs={{0,16},{1,9},{2,18},{3,11},{4,20},{5,13},{6,22},{7,15},{8,24},{9,1... | collective-permute-start | bytes 7471112 | tf_op jit(solution)/shard_map/ppermute | solution.py:403
  (58 other events, 573.0 us)
